TPU v7x, 512 devices: a whole 4x4x16 slice. The times are simulated.
512 devices in a mesh: row: 16 (over x, y), col: 16 (over z_lo, core), cfg: 2 (over z_hi).
Axes of the slice: x: 4, y: 4, z: 16 (z_hi: 2, z_lo: 8; z = z_hi * 8 + z_lo), core: 2. Of those that a mesh axis runs over, the one named last changes fastest.
Arguments:
- features: bfloat16 [2, 192, 1024, 320], P('cfg', 'row', 'col'), may hold values from -6 to 6
- latent: float32 [4, 192, 1024], P('cfg', 'row', 'col'), may hold values from -6 to 6
- conv_weight: bfloat16 [2, 2, 9, 320, 320], replicated, may hold values from -0.109375 to 0.109375
- conv_bias: float32 [2, 2, 320], replicated, may hold values from -2 to 2
- norm_gain: float32 [5, 320], replicated, may hold values from 0.5 to 1.5
- norm_shift: float32 [5, 320], replicated, may hold values from -2 to 2
- emb_shift: float32 [2, 2, 320], P('cfg'), may hold values from -5 to 5
- stale_mean: float32 [2, 5, 32], P('cfg'), may hold values from -2 to 2
- stale_var: float32 [2, 5, 32], P('cfg'), may hold values from 0.3 to 3
- out_weight: bfloat16 [9, 320, 4], replicated, may hold values from -0.109375 to 0.109375
- out_bias: float32 [4], replicated, may hold values from -2 to 2
- guidance: float32 [1], replicated, may hold values from 2 to 6
- timestep: int32 [1], replicated, may hold values from 0 to 49
- coeffs: float32 [50, 2], replicated, may hold values from 0.5 to 1.5
Outputs:
- latent_next: float32 [4, 192, 1024], P('cfg', 'row', 'col')
Inputs may be any that keep to these rules, and one draw needn't show every extreme that they name: `timestep`: the row of coeffs used in this step.
All inputs are finite; a program needn't handle non-finite values.
Results may differ from a plain program's by a relative error of at most 0.02.
Values may be sent and summed in bfloat16 or wider, within the bound.
A program may use at most 64 MiB of HBM per device.

v0:
```python
import jax
import jax.numpy as jnp
from jax import lax
from jax.sharding import PartitionSpec as P

BLOCKS = 2


norm_eps = 1e-05


def extended(block, sides, width):
    for axis, dim in sides:
        count = lax.axis_size(axis)
        forward = [(i, i + 1) for i in range(count - 1)]
        backward = [(target, source) for source, target in forward]
        low = lax.ppermute(
            lax.slice_in_dim(block, block.shape[dim] - width, None, axis=dim), axis, forward
        )
        high = lax.ppermute(lax.slice_in_dim(block, 0, width, axis=dim), axis, backward)
        block = jnp.concatenate([low, block, high], axis=dim)
    return block


def partner_2(value, axis, distance):
    mask = 2**distance
    pairs = [(source, source ^ mask) for source in range(lax.axis_size(axis))]
    return lax.ppermute(value, axis, pairs)


def activate(values, index, group_mean, group_var, norm_gain, norm_shift):
    channels = values.shape[-1]
    repeat_by = channels // group_mean.shape[-1]
    centre = jnp.repeat(group_mean[index], repeat_by)
    scaling = jnp.repeat(lax.rsqrt(group_var[index] + norm_eps), repeat_by)
    normed = (values.astype(jnp.float32) - centre) * scaling * norm_gain[index] + norm_shift[index]
    return jax.nn.silu(normed)


def conv_valid(padded, kernel):
    row_count = padded.shape[0] - 2
    col_count = padded.shape[1] - 2
    channels = padded.shape[2]
    summed = None
    for tap_index in range(9):
        tap_row, tap_col = divmod(tap_index, 3)
        window = padded[tap_row : tap_row + row_count, tap_col : tap_col + col_count].reshape(
            row_count * col_count, channels
        )
        product = jnp.dot(window, kernel[tap_index], preferred_element_type=jnp.float32)
        summed = product if summed is None else summed + product
    return summed.reshape(row_count, col_count, kernel.shape[2])


def pad_one(tile_act):
    return extended(tile_act, (("row", 0), ("col", 1)), 1)


def conv_layer(tile_act, kernel):
    padded = pad_one(tile_act)
    return conv_valid(padded, kernel)


def per_device(
    features,
    latent,
    conv_weight,
    conv_bias,
    norm_gain,
    norm_shift,
    emb_shift,
    stale_mean,
    stale_var,
    out_weight,
    out_bias,
    guidance,
    timestep,
    coeffs,
):
    hidden = features[0]
    group_mean = stale_mean[0]
    group_var = stale_var[0]
    branch_shift = emb_shift[0]
    for block_index in range(BLOCKS):
        first_act = activate(
            hidden, 2 * block_index, group_mean, group_var, norm_gain, norm_shift
        ).astype(jnp.bfloat16)
        inner_sum = (
            conv_layer(first_act, conv_weight[block_index, 0])
            + conv_bias[block_index, 0]
            + branch_shift[block_index]
        )
        second = activate(
            inner_sum, 2 * block_index + 1, group_mean, group_var, norm_gain, norm_shift
        ).astype(jnp.bfloat16)
        conv_two = conv_layer(second, conv_weight[block_index, 1]) + conv_bias[block_index, 1]
        hidden = (hidden.astype(jnp.float32) + conv_two).astype(jnp.bfloat16)
    final_act = activate(hidden, 2 * BLOCKS, group_mean, group_var, norm_gain, norm_shift).astype(
        jnp.bfloat16
    )
    noise_pred = jnp.transpose(conv_layer(final_act, out_weight) + out_bias, (2, 0, 1))
    half_lat = latent.shape[0]
    branch_id = lax.axis_index("cfg")
    own_part = lax.dynamic_slice_in_dim(noise_pred, branch_id * half_lat, half_lat, 0)
    other_part = lax.dynamic_slice_in_dim(noise_pred, (1 - branch_id) * half_lat, half_lat, 0)
    partner = partner_2(other_part, "cfg", 0)
    is_cond = branch_id == 1
    uncond = jnp.where(is_cond, partner, own_part)
    conditioned = jnp.where(is_cond, own_part, partner)
    guided = uncond + guidance[0] * (conditioned - uncond)
    step_coef = coeffs[timestep[0]]
    return step_coef[0] * latent + step_coef[1] * guided


def solution(mesh):
    return jax.shard_map(
        per_device,
        mesh=mesh,
        in_specs=(
            P("cfg", "row", "col", None),
            P("cfg", "row", "col"),
            P(),
            P(),
            P(),
            P(),
            P("cfg", None, None),
            P("cfg", None, None),
            P("cfg", None, None),
            P(),
            P(),
            P(),
            P(),
            P(),
        ),
        out_specs=P("cfg", "row", "col"),
        check_vma=False,
    )
```

profile of v0, /device:TPU:123, one launch (start us, length us, event | category | flops | bytes accessed | tf_op | source)
XLA Modules:
  0.0 176.0 jit_solution(16899536462832246748)
XLA Ops:
  3.0 1.5 multiply_convert_fusion.4
  4.5 2.8 %collective-permute-start = (bf16[1,64,320]{2,1,0:T(8,128)(2,1)S(1)}, bf16[1,64,320]{2,1,0:T(8,128)(2,1)S(1)}, u32[]{:S(2)}, u32[]{:S(2)}) collective-permute-start(bf16[1,64,320]{2,1,0:T(8,128)(2,1)S(1)} %get-tuple-element.91), channel_id=1, source_target_pairs={{0,32},{32,64},{64,96},{96,128},{128,160},{160,192},{192,224},{224... | collective-permute-start | bytes 122888 | tf_op jit(solution)/shard_map/ppermute | solution.py:17
  7.3 2.5 %collective-permute-start.1 = (bf16[1,64,320]{2,1,0:T(8,128)(2,1)S(1)}, bf16[1,64,320]{2,1,0:T(8,128)(2,1)S(1)}, u32[]{:S(2)}, u32[]{:S(2)}) collective-permute-start(bf16[1,64,320]{2,1,0:T(8,128)(2,1)S(1)} %get-tuple-element.92), channel_id=1, source_target_pairs={{32,0},{64,32},{96,64},{128,96},{160,128},{192,160},{224,192},{256... | collective-permute-start | bytes 122888 | tf_op jit(solution)/shard_map/ppermute | solution.py:20
  10.7 3.6 %collective-permute-done.1 = bf16[1,64,320]{2,1,0:T(8,128)(2,1)S(1)} collective-permute-done((bf16[1,64,320]{2,1,0:T(8,128)(2,1)S(1)}, bf16[1,64,320]{2,1,0:T(8,128)(2,1)S(1)}, u32[]{:S(2)}, u32[]{:S(2)}) %collective-permute-start.1) | collective-permute-done | bytes 40992 | tf_op jit(solution)/shard_map/ppermute | solution.py:20
  14.3 6.7 %collective-permute-start.2 = (bf16[14,1,320]{2,1,0:T(2,128)(2,1)S(1)}, bf16[14,1,320]{2,1,0:T(2,128)(2,1)S(1)}, u32[]{:S(2)}, u32[]{:S(2)}) collective-permute-start(bf16[14,1,320]{2,1,0:T(2,128)(2,1)S(1)} %get-tuple-element.71), channel_id=1, source_target_pairs={{0,2},{2,4},{4,6},{6,8},{8,10},{10,12},{12,14},{14,16},{16,18},{18... | collective-permute-start | bytes 26888 | tf_op jit(solution)/shard_map/ppermute | solution.py:17
  21.0 1.9 %collective-permute-start.3 = (bf16[14,1,320]{2,1,0:T(2,128)(2,1)S(1)}, bf16[14,1,320]{2,1,0:T(2,128)(2,1)S(1)}, u32[]{:S(2)}, u32[]{:S(2)}) collective-permute-start(bf16[14,1,320]{2,1,0:T(2,128)(2,1)S(1)} %get-tuple-element.72), channel_id=1, source_target_pairs={{2,0},{4,2},{6,4},{8,6},{10,8},{12,10},{14,12},{16,14},{18,16},{20... | collective-permute-start | bytes 26888 | tf_op jit(solution)/shard_map/ppermute | solution.py:20
  23.1 1.4 fusion.90
  24.6 2.8 %collective-permute-done.3 = bf16[14,1,320]{2,1,0:T(2,128)(2,1)S(1)} collective-permute-done((bf16[14,1,320]{2,1,0:T(2,128)(2,1)S(1)}, bf16[14,1,320]{2,1,0:T(2,128)(2,1)S(1)}, u32[]{:S(2)}, u32[]{:S(2)}) %collective-permute-start.3) | collective-permute-done | bytes 8992 | tf_op jit(solution)/shard_map/ppermute | solution.py:20
  28.3 1.4 fusion.82
  29.7 1.4 convolution_add_fusion.27
  31.1 1.4 convolution_add_fusion.26
  32.6 1.4 convolution_add_fusion.25
  34.0 1.4 convolution_add_fusion.24
  35.4 1.4 convolution_add_fusion.23
  36.9 1.4 convolution_add_fusion.22
  38.3 1.4 fusion.3
  40.6 1.9 %collective-permute-start.4 = (bf16[1,64,320]{2,1,0:T(8,128)(2,1)S(1)}, bf16[1,64,320]{2,1,0:T(8,128)(2,1)S(1)}, u32[]{:S(2)}, u32[]{:S(2)}) collective-permute-start(bf16[1,64,320]{2,1,0:T(8,128)(2,1)S(1)} %get-tuple-element.87), channel_id=1, source_target_pairs={{0,32},{32,64},{64,96},{96,128},{128,160},{160,192},{192,224},{224... | collective-permute-start | bytes 122888 | tf_op jit(solution)/shard_map/ppermute | solution.py:17
  42.5 3.4 %collective-permute-start.5 = (bf16[1,64,320]{2,1,0:T(8,128)(2,1)S(1)}, bf16[1,64,320]{2,1,0:T(8,128)(2,1)S(1)}, u32[]{:S(2)}, u32[]{:S(2)}) collective-permute-start(bf16[1,64,320]{2,1,0:T(8,128)(2,1)S(1)} %get-tuple-element.88), channel_id=1, source_target_pairs={{32,0},{64,32},{96,64},{128,96},{160,128},{192,160},{224,192},{256... | collective-permute-start | bytes 122888 | tf_op jit(solution)/shard_map/ppermute | solution.py:20
  46.5 3.0 %collective-permute-done.5 = bf16[1,64,320]{2,1,0:T(8,128)(2,1)S(1)} collective-permute-done((bf16[1,64,320]{2,1,0:T(8,128)(2,1)S(1)}, bf16[1,64,320]{2,1,0:T(8,128)(2,1)S(1)}, u32[]{:S(2)}, u32[]{:S(2)}) %collective-permute-start.5) | collective-permute-done | bytes 40992 | tf_op jit(solution)/shard_map/ppermute | solution.py:20
  49.5 3.4 %collective-permute-start.6 = (bf16[14,1,320]{2,1,0:T(2,128)(2,1)S(1)}, bf16[14,1,320]{2,1,0:T(2,128)(2,1)S(1)}, u32[]{:S(2)}, u32[]{:S(2)}) collective-permute-start(bf16[14,1,320]{2,1,0:T(2,128)(2,1)S(1)} %get-tuple-element.67), channel_id=1, source_target_pairs={{0,2},{2,4},{4,6},{6,8},{8,10},{10,12},{12,14},{14,16},{16,18},{18... | collective-permute-start | bytes 26888 | tf_op jit(solution)/shard_map/ppermute | solution.py:17
  53.0 2.1 %collective-permute-start.7 = (bf16[14,1,320]{2,1,0:T(2,128)(2,1)S(1)}, bf16[14,1,320]{2,1,0:T(2,128)(2,1)S(1)}, u32[]{:S(2)}, u32[]{:S(2)}) collective-permute-start(bf16[14,1,320]{2,1,0:T(2,128)(2,1)S(1)} %get-tuple-element.68), channel_id=1, source_target_pairs={{2,0},{4,2},{6,4},{8,6},{10,8},{12,10},{14,12},{16,14},{18,16},{20... | collective-permute-start | bytes 26888 | tf_op jit(solution)/shard_map/ppermute | solution.py:20
  56.7 2.6 %collective-permute-done.7 = bf16[14,1,320]{2,1,0:T(2,128)(2,1)S(1)} collective-permute-done((bf16[14,1,320]{2,1,0:T(2,128)(2,1)S(1)}, bf16[14,1,320]{2,1,0:T(2,128)(2,1)S(1)}, u32[]{:S(2)}, u32[]{:S(2)}) %collective-permute-start.7) | collective-permute-done | bytes 8992 | tf_op jit(solution)/shard_map/ppermute | solution.py:20
  60.2 1.4 convolution_add_fusion.20
  61.7 1.4 convolution_add_fusion.19
  63.1 1.4 convolution_add_fusion.18
  64.5 1.8 %convolution_add_fusion.17 = f32[768,320]{0,1:T(8,128)S(1)} fusion(f32[768,320]{0,1:T(8,128)S(1)} %convolution_add_fusion.18, f32[768,320]{0,1:T(8,128)S(1)} %fusion.3, f32[320]{0:T(512)S(1)} %get-tuple-element.12, f32[320]{0:T(512)S(1)} %get-tuple-element.109, f32[320]{0:T(512)S(1)} %mul.223, f32[320]{0:T(512)S(1)} %sub.87, ...), kind=kOutput, calls=%fused_computation.22 | convolution fusion | flops 160235520 | bytes 3202560 | tf_op jit(solution)/shard_map/dot_general | solution.py:50
  67.7 1.4 convolution_add_fusion.16
  69.2 1.4 convolution_add_fusion.15
  70.6 2.3 %add_convert_fusion = (bf16[768,320]{0,1:T(8,128)(2,1)}, f32[768,320]{0,1:T(8,128)S(1)}) fusion(f32[768,320]{0,1:T(8,128)S(1)} %copy.24, f32[320]{0:T(512)S(1)} %get-tuple-element.16, f32[768,320]{0,1:T(8,128)S(1)} %fusion.71, f32[768,320]{0,1:T(8,128)S(1)} %convolution_add_fusion.15, bf16[768,320]{1,0:T(8,128)(2,1)S(1)} %bitcast.291, ...), kind=kOutput, calls=%fused_computation.77 | convolution fusion | flops 158515200 | bytes 5162240 | tf_op jit(solution)/shard_map/dot_general | solution.py:50
  73.8 1.9 %collective-permute-start.8 = (bf16[1,64,320]{2,1,0:T(8,128)(2,1)S(1)}, bf16[1,64,320]{2,1,0:T(8,128)(2,1)S(1)}, u32[]{:S(2)}, u32[]{:S(2)}) collective-permute-start(bf16[1,64,320]{2,1,0:T(8,128)(2,1)S(1)} %get-tuple-element.83), channel_id=1, source_target_pairs={{0,32},{32,64},{64,96},{96,128},{128,160},{160,192},{192,224},{224... | collective-permute-start | bytes 122888 | tf_op jit(solution)/shard_map/ppermute | solution.py:17
  75.7 3.4 %collective-permute-start.9 = (bf16[1,64,320]{2,1,0:T(8,128)(2,1)S(1)}, bf16[1,64,320]{2,1,0:T(8,128)(2,1)S(1)}, u32[]{:S(2)}, u32[]{:S(2)}) collective-permute-start(bf16[1,64,320]{2,1,0:T(8,128)(2,1)S(1)} %get-tuple-element.84), channel_id=1, source_target_pairs={{32,0},{64,32},{96,64},{128,96},{160,128},{192,160},{224,192},{256... | collective-permute-start | bytes 122888 | tf_op jit(solution)/shard_map/ppermute | solution.py:20
  79.5 3.2 %collective-permute-done.9 = bf16[1,64,320]{2,1,0:T(8,128)(2,1)S(1)} collective-permute-done((bf16[1,64,320]{2,1,0:T(8,128)(2,1)S(1)}, bf16[1,64,320]{2,1,0:T(8,128)(2,1)S(1)}, u32[]{:S(2)}, u32[]{:S(2)}) %collective-permute-start.9) | collective-permute-done | bytes 40992 | tf_op jit(solution)/shard_map/ppermute | solution.py:20
  82.7 3.4 %collective-permute-start.10 = (bf16[14,1,320]{2,1,0:T(2,128)(2,1)S(1)}, bf16[14,1,320]{2,1,0:T(2,128)(2,1)S(1)}, u32[]{:S(2)}, u32[]{:S(2)}) collective-permute-start(bf16[14,1,320]{2,1,0:T(2,128)(2,1)S(1)} %get-tuple-element.63), channel_id=1, source_target_pairs={{0,2},{2,4},{4,6},{6,8},{8,10},{10,12},{12,14},{14,16},{16,18},{18... | collective-permute-start | bytes 26888 | tf_op jit(solution)/shard_map/ppermute | solution.py:17
  86.1 1.9 %collective-permute-start.11 = (bf16[14,1,320]{2,1,0:T(2,128)(2,1)S(1)}, bf16[14,1,320]{2,1,0:T(2,128)(2,1)S(1)}, u32[]{:S(2)}, u32[]{:S(2)}) collective-permute-start(bf16[14,1,320]{2,1,0:T(2,128)(2,1)S(1)} %get-tuple-element.64), channel_id=1, source_target_pairs={{2,0},{4,2},{6,4},{8,6},{10,8},{12,10},{14,12},{16,14},{18,16},{20... | collective-permute-start | bytes 26888 | tf_op jit(solution)/shard_map/ppermute | solution.py:20
  89.7 2.8 %collective-permute-done.11 = bf16[14,1,320]{2,1,0:T(2,128)(2,1)S(1)} collective-permute-done((bf16[14,1,320]{2,1,0:T(2,128)(2,1)S(1)}, bf16[14,1,320]{2,1,0:T(2,128)(2,1)S(1)}, u32[]{:S(2)}, u32[]{:S(2)}) %collective-permute-start.11) | collective-permute-done | bytes 8992 | tf_op jit(solution)/shard_map/ppermute | solution.py:20
  94.8 1.4 convolution_add_fusion.13
  96.2 1.4 convolution_add_fusion.12
  97.7 1.5 convolution_add_fusion.11
  99.2 1.7 convolution_add_fusion.10
  100.9 1.4 convolution_add_fusion.9
  102.3 1.4 convolution_add_fusion.8
  103.8 1.4 fusion.1
  106.1 2.1 %collective-permute-start.12 = (bf16[1,64,320]{2,1,0:T(8,128)(2,1)S(1)}, bf16[1,64,320]{2,1,0:T(8,128)(2,1)S(1)}, u32[]{:S(2)}, u32[]{:S(2)}) collective-permute-start(bf16[1,64,320]{2,1,0:T(8,128)(2,1)S(1)} %get-tuple-element.79), channel_id=1, source_target_pairs={{0,32},{32,64},{64,96},{96,128},{128,160},{160,192},{192,224},{224... | collective-permute-start | bytes 122888 | tf_op jit(solution)/shard_map/ppermute | solution.py:17
  108.2 3.4 %collective-permute-start.13 = (bf16[1,64,320]{2,1,0:T(8,128)(2,1)S(1)}, bf16[1,64,320]{2,1,0:T(8,128)(2,1)S(1)}, u32[]{:S(2)}, u32[]{:S(2)}) collective-permute-start(bf16[1,64,320]{2,1,0:T(8,128)(2,1)S(1)} %get-tuple-element.80), channel_id=1, source_target_pairs={{32,0},{64,32},{96,64},{128,96},{160,128},{192,160},{224,192},{256... | collective-permute-start | bytes 122888 | tf_op jit(solution)/shard_map/ppermute | solution.py:20
  112.6 2.5 %collective-permute-done.13 = bf16[1,64,320]{2,1,0:T(8,128)(2,1)S(1)} collective-permute-done((bf16[1,64,320]{2,1,0:T(8,128)(2,1)S(1)}, bf16[1,64,320]{2,1,0:T(8,128)(2,1)S(1)}, u32[]{:S(2)}, u32[]{:S(2)}) %collective-permute-start.13) | collective-permute-done | bytes 40992 | tf_op jit(solution)/shard_map/ppermute | solution.py:20
  115.2 3.2 %collective-permute-start.14 = (bf16[14,1,320]{2,1,0:T(2,128)(2,1)S(1)}, bf16[14,1,320]{2,1,0:T(2,128)(2,1)S(1)}, u32[]{:S(2)}, u32[]{:S(2)}) collective-permute-start(bf16[14,1,320]{2,1,0:T(2,128)(2,1)S(1)} %get-tuple-element.59), channel_id=1, source_target_pairs={{0,2},{2,4},{4,6},{6,8},{8,10},{10,12},{12,14},{14,16},{16,18},{18... | collective-permute-start | bytes 26888 | tf_op jit(solution)/shard_map/ppermute | solution.py:17
  118.4 1.9 %collective-permute-start.15 = (bf16[14,1,320]{2,1,0:T(2,128)(2,1)S(1)}, bf16[14,1,320]{2,1,0:T(2,128)(2,1)S(1)}, u32[]{:S(2)}, u32[]{:S(2)}) collective-permute-start(bf16[14,1,320]{2,1,0:T(2,128)(2,1)S(1)} %get-tuple-element.60), channel_id=1, source_target_pairs={{2,0},{4,2},{6,4},{8,6},{10,8},{12,10},{14,12},{16,14},{18,16},{20... | collective-permute-start | bytes 26888 | tf_op jit(solution)/shard_map/ppermute | solution.py:20
  120.6 1.4 fusion.57
  122.0 2.8 %collective-permute-done.15 = bf16[14,1,320]{2,1,0:T(2,128)(2,1)S(1)} collective-permute-done((bf16[14,1,320]{2,1,0:T(2,128)(2,1)S(1)}, bf16[14,1,320]{2,1,0:T(2,128)(2,1)S(1)}, u32[]{:S(2)}, u32[]{:S(2)}) %collective-permute-start.15) | collective-permute-done | bytes 8992 | tf_op jit(solution)/shard_map/ppermute | solution.py:20
  125.7 1.4 convolution_add_fusion.6
  127.2 1.4 convolution_add_fusion.5
  128.6 1.4 convolution_add_fusion.4
  130.0 1.8 %convolution_add_fusion.3 = f32[768,320]{0,1:T(8,128)S(1)} fusion(f32[768,320]{0,1:T(8,128)S(1)} %convolution_add_fusion.4, f32[768,320]{0,1:T(8,128)S(1)} %fusion.1, f32[320]{0:T(512)S(1)} %get-tuple-element.14, f32[320]{0:T(512)S(1)} %get-tuple-element.107, f32[320]{0:T(512)S(1)} %mul.247, f32[320]{0:T(512)S(1)} %sub.97, f32[320]{0:T(512)S(1)} %get-tuple-element.113, ...), kind=kOutput, calls=%fused_computation.6 | convolution fusion | flops 160235520 | bytes 3202560 | tf_op jit(solution)/shard_map/dot_general | solution.py:50
  133.2 1.4 convolution_add_fusion.2
  134.6 1.4 convolution_add_fusion.1
  136.1 1.4 fusion
  138.4 1.9 %collective-permute-start.16 = (bf16[1,64,320]{2,1,0:T(8,128)(2,1)S(1)}, bf16[1,64,320]{2,1,0:T(8,128)(2,1)S(1)}, u32[]{:S(2)}, u32[]{:S(2)}) collective-permute-start(bf16[1,64,320]{2,1,0:T(8,128)(2,1)S(1)} %get-tuple-element.75), channel_id=1, source_target_pairs={{0,32},{32,64},{64,96},{96,128},{128,160},{160,192},{192,224},{224... | collective-permute-start | bytes 122888 | tf_op jit(solution)/shard_map/ppermute | solution.py:17
  140.4 3.4 %collective-permute-start.17 = (bf16[1,64,320]{2,1,0:T(8,128)(2,1)S(1)}, bf16[1,64,320]{2,1,0:T(8,128)(2,1)S(1)}, u32[]{:S(2)}, u32[]{:S(2)}) collective-permute-start(bf16[1,64,320]{2,1,0:T(8,128)(2,1)S(1)} %get-tuple-element.76), channel_id=1, source_target_pairs={{32,0},{64,32},{96,64},{128,96},{160,128},{192,160},{224,192},{256... | collective-permute-start | bytes 122888 | tf_op jit(solution)/shard_map/ppermute | solution.py:20
  143.8 3.5 %collective-permute-done.17 = bf16[1,64,320]{2,1,0:T(8,128)(2,1)S(1)} collective-permute-done((bf16[1,64,320]{2,1,0:T(8,128)(2,1)S(1)}, bf16[1,64,320]{2,1,0:T(8,128)(2,1)S(1)}, u32[]{:S(2)}, u32[]{:S(2)}) %collective-permute-start.17) | collective-permute-done | bytes 40992 | tf_op jit(solution)/shard_map/ppermute | solution.py:20
  147.3 3.2 %collective-permute-start.18 = (bf16[14,1,320]{2,1,0:T(2,128)(2,1)S(1)}, bf16[14,1,320]{2,1,0:T(2,128)(2,1)S(1)}, u32[]{:S(2)}, u32[]{:S(2)}) collective-permute-start(bf16[14,1,320]{2,1,0:T(2,128)(2,1)S(1)} %get-tuple-element.55), channel_id=1, source_target_pairs={{0,2},{2,4},{4,6},{6,8},{8,10},{10,12},{12,14},{14,16},{16,18},{18... | collective-permute-start | bytes 26888 | tf_op jit(solution)/shard_map/ppermute | solution.py:17
  150.6 1.9 %collective-permute-start.19 = (bf16[14,1,320]{2,1,0:T(2,128)(2,1)S(1)}, bf16[14,1,320]{2,1,0:T(2,128)(2,1)S(1)}, u32[]{:S(2)}, u32[]{:S(2)}) collective-permute-start(bf16[14,1,320]{2,1,0:T(2,128)(2,1)S(1)} %get-tuple-element.56), channel_id=1, source_target_pairs={{2,0},{4,2},{6,4},{8,6},{10,8},{12,10},{14,12},{16,14},{18,16},{20... | collective-permute-start | bytes 26888 | tf_op jit(solution)/shard_map/ppermute | solution.py:20
  152.9 3.9 %collective-permute-done.19 = bf16[14,1,320]{2,1,0:T(2,128)(2,1)S(1)} collective-permute-done((bf16[14,1,320]{2,1,0:T(2,128)(2,1)S(1)}, bf16[14,1,320]{2,1,0:T(2,128)(2,1)S(1)}, u32[]{:S(2)}, u32[]{:S(2)}) %collective-permute-start.19) | collective-permute-done | bytes 8992 | tf_op jit(solution)/shard_map/ppermute | solution.py:20
  160.9 10.4 %collective-permute-start.20 = (f32[2,12,64]{2,1,0:T(8,128)S(1)}, f32[2,12,64]{2,1,0:T(8,128)S(1)}, u32[]{:S(2)}, u32[]{:S(2)}) collective-permute-start(f32[2,12,64]{2,1,0:T(8,128)S(1)} %dynamic-slice_bitcast_fusion), channel_id=1, source_target_pairs={{0,1},{1,0},{2,3},{3,2},{4,5},{5,4},{6,7},{7,6},{8,9},{9,8},{10,11... | collective-permute-start | bytes 18440 | tf_op jit(solution)/shard_map/ppermute | solution.py:28
  172.6 1.5 collective-permute-done.20
  (113 shorter events, 27.2 us)
Async XLA Ops:
  0.0 143.7 %copy-start = (f32[50,2]{0,1:T(2,128)S(1)}, f32[50,2]{0,1:T(2,128)}, u32[]{:S(2)}) copy-start(f32[50,2]{0,1:T(2,128)} %param.27) | copy-start | bytes 1204
  0.0 9.8 %copy-start.1 = (bf16[1,12,64,320]{3,2,1,0:T(8,128)(2,1)S(1)}, bf16[1,12,64,320]{3,2,1,0:T(8,128)(2,1)}, u32[]{:S(2)}) copy-start(bf16[1,12,64,320]{3,2,1,0:T(8,128)(2,1)} %param.14) | copy-start | bytes 1474564
  0.0 10.2 %copy-start.6 = (f32[2,2,320]{2,1,0:T(2,128)S(1)}, f32[2,2,320]{2,1,0:T(2,128)}, u32[]{:S(2)}) copy-start(f32[2,2,320]{2,1,0:T(2,128)} %param.17) | copy-start | bytes 15364
  0.0 10.2 %copy-start.7 = (f32[1,2,320]{2,1,0:T(2,128)S(1)}, f32[1,2,320]{2,1,0:T(2,128)}, u32[]{:S(2)}) copy-start(f32[1,2,320]{2,1,0:T(2,128)} %param.20) | copy-start | bytes 7684
  4.5 6.2 %collective-permute-start = (bf16[1,64,320]{2,1,0:T(8,128)(2,1)S(1)}, bf16[1,64,320]{2,1,0:T(8,128)(2,1)S(1)}, u32[]{:S(2)}, u32[]{:S(2)}) collective-permute-start(bf16[1,64,320]{2,1,0:T(8,128)(2,1)S(1)} %get-tuple-element.91), channel_id=1, source_target_pairs={{0,32},{32,64},{64,96},{96,128},{128,160},{160,192},{192,224},{224... | collective-permute-start | bytes 122888 | tf_op jit(solution)/shard_map/ppermute | solution.py:17
  7.3 6.9 %collective-permute-start.1 = (bf16[1,64,320]{2,1,0:T(8,128)(2,1)S(1)}, bf16[1,64,320]{2,1,0:T(8,128)(2,1)S(1)}, u32[]{:S(2)}, u32[]{:S(2)}) collective-permute-start(bf16[1,64,320]{2,1,0:T(8,128)(2,1)S(1)} %get-tuple-element.92), channel_id=1, source_target_pairs={{32,0},{64,32},{96,64},{128,96},{160,128},{192,160},{224,192},{256... | collective-permute-start | bytes 122888 | tf_op jit(solution)/shard_map/ppermute | solution.py:20
  14.3 10.3 %collective-permute-start.2 = (bf16[14,1,320]{2,1,0:T(2,128)(2,1)S(1)}, bf16[14,1,320]{2,1,0:T(2,128)(2,1)S(1)}, u32[]{:S(2)}, u32[]{:S(2)}) collective-permute-start(bf16[14,1,320]{2,1,0:T(2,128)(2,1)S(1)} %get-tuple-element.71), channel_id=1, source_target_pairs={{0,2},{2,4},{4,6},{6,8},{8,10},{10,12},{12,14},{14,16},{16,18},{18... | collective-permute-start | bytes 26888 | tf_op jit(solution)/shard_map/ppermute | solution.py:17
  21.0 6.3 %collective-permute-start.3 = (bf16[14,1,320]{2,1,0:T(2,128)(2,1)S(1)}, bf16[14,1,320]{2,1,0:T(2,128)(2,1)S(1)}, u32[]{:S(2)}, u32[]{:S(2)}) collective-permute-start(bf16[14,1,320]{2,1,0:T(2,128)(2,1)S(1)} %get-tuple-element.72), channel_id=1, source_target_pairs={{2,0},{4,2},{6,4},{8,6},{10,8},{12,10},{14,12},{16,14},{18,16},{20... | collective-permute-start | bytes 26888 | tf_op jit(solution)/shard_map/ppermute | solution.py:20
  40.6 5.9 %collective-permute-start.4 = (bf16[1,64,320]{2,1,0:T(8,128)(2,1)S(1)}, bf16[1,64,320]{2,1,0:T(8,128)(2,1)S(1)}, u32[]{:S(2)}, u32[]{:S(2)}) collective-permute-start(bf16[1,64,320]{2,1,0:T(8,128)(2,1)S(1)} %get-tuple-element.87), channel_id=1, source_target_pairs={{0,32},{32,64},{64,96},{96,128},{128,160},{160,192},{192,224},{224... | collective-permute-start | bytes 122888 | tf_op jit(solution)/shard_map/ppermute | solution.py:17
  42.5 6.9 %collective-permute-start.5 = (bf16[1,64,320]{2,1,0:T(8,128)(2,1)S(1)}, bf16[1,64,320]{2,1,0:T(8,128)(2,1)S(1)}, u32[]{:S(2)}, u32[]{:S(2)}) collective-permute-start(bf16[1,64,320]{2,1,0:T(8,128)(2,1)S(1)} %get-tuple-element.88), channel_id=1, source_target_pairs={{32,0},{64,32},{96,64},{128,96},{160,128},{192,160},{224,192},{256... | collective-permute-start | bytes 122888 | tf_op jit(solution)/shard_map/ppermute | solution.py:20
  49.5 7.2 %collective-permute-start.6 = (bf16[14,1,320]{2,1,0:T(2,128)(2,1)S(1)}, bf16[14,1,320]{2,1,0:T(2,128)(2,1)S(1)}, u32[]{:S(2)}, u32[]{:S(2)}) collective-permute-start(bf16[14,1,320]{2,1,0:T(2,128)(2,1)S(1)} %get-tuple-element.67), channel_id=1, source_target_pairs={{0,2},{2,4},{4,6},{6,8},{8,10},{10,12},{12,14},{14,16},{16,18},{18... | collective-permute-start | bytes 26888 | tf_op jit(solution)/shard_map/ppermute | solution.py:17
  53.0 6.3 %collective-permute-start.7 = (bf16[14,1,320]{2,1,0:T(2,128)(2,1)S(1)}, bf16[14,1,320]{2,1,0:T(2,128)(2,1)S(1)}, u32[]{:S(2)}, u32[]{:S(2)}) collective-permute-start(bf16[14,1,320]{2,1,0:T(2,128)(2,1)S(1)} %get-tuple-element.68), channel_id=1, source_target_pairs={{2,0},{4,2},{6,4},{8,6},{10,8},{12,10},{14,12},{16,14},{18,16},{20... | collective-permute-start | bytes 26888 | tf_op jit(solution)/shard_map/ppermute | solution.py:20
  73.8 5.7 %collective-permute-start.8 = (bf16[1,64,320]{2,1,0:T(8,128)(2,1)S(1)}, bf16[1,64,320]{2,1,0:T(8,128)(2,1)S(1)}, u32[]{:S(2)}, u32[]{:S(2)}) collective-permute-start(bf16[1,64,320]{2,1,0:T(8,128)(2,1)S(1)} %get-tuple-element.83), channel_id=1, source_target_pairs={{0,32},{32,64},{64,96},{96,128},{128,160},{160,192},{192,224},{224... | collective-permute-start | bytes 122888 | tf_op jit(solution)/shard_map/ppermute | solution.py:17
  75.7 6.9 %collective-permute-start.9 = (bf16[1,64,320]{2,1,0:T(8,128)(2,1)S(1)}, bf16[1,64,320]{2,1,0:T(8,128)(2,1)S(1)}, u32[]{:S(2)}, u32[]{:S(2)}) collective-permute-start(bf16[1,64,320]{2,1,0:T(8,128)(2,1)S(1)} %get-tuple-element.84), channel_id=1, source_target_pairs={{32,0},{64,32},{96,64},{128,96},{160,128},{192,160},{224,192},{256... | collective-permute-start | bytes 122888 | tf_op jit(solution)/shard_map/ppermute | solution.py:20
  82.7 6.9 %collective-permute-start.10 = (bf16[14,1,320]{2,1,0:T(2,128)(2,1)S(1)}, bf16[14,1,320]{2,1,0:T(2,128)(2,1)S(1)}, u32[]{:S(2)}, u32[]{:S(2)}) collective-permute-start(bf16[14,1,320]{2,1,0:T(2,128)(2,1)S(1)} %get-tuple-element.63), channel_id=1, source_target_pairs={{0,2},{2,4},{4,6},{6,8},{8,10},{10,12},{12,14},{14,16},{16,18},{18... | collective-permute-start | bytes 26888 | tf_op jit(solution)/shard_map/ppermute | solution.py:17
  86.1 6.3 %collective-permute-start.11 = (bf16[14,1,320]{2,1,0:T(2,128)(2,1)S(1)}, bf16[14,1,320]{2,1,0:T(2,128)(2,1)S(1)}, u32[]{:S(2)}, u32[]{:S(2)}) collective-permute-start(bf16[14,1,320]{2,1,0:T(2,128)(2,1)S(1)} %get-tuple-element.64), channel_id=1, source_target_pairs={{2,0},{4,2},{6,4},{8,6},{10,8},{12,10},{14,12},{16,14},{18,16},{20... | collective-permute-start | bytes 26888 | tf_op jit(solution)/shard_map/ppermute | solution.py:20
  97.7 1.5 copy-start.2
  106.1 6.5 %collective-permute-start.12 = (bf16[1,64,320]{2,1,0:T(8,128)(2,1)S(1)}, bf16[1,64,320]{2,1,0:T(8,128)(2,1)S(1)}, u32[]{:S(2)}, u32[]{:S(2)}) collective-permute-start(bf16[1,64,320]{2,1,0:T(8,128)(2,1)S(1)} %get-tuple-element.79), channel_id=1, source_target_pairs={{0,32},{32,64},{64,96},{96,128},{128,160},{160,192},{192,224},{224... | collective-permute-start | bytes 122888 | tf_op jit(solution)/shard_map/ppermute | solution.py:17
  108.2 6.9 %collective-permute-start.13 = (bf16[1,64,320]{2,1,0:T(8,128)(2,1)S(1)}, bf16[1,64,320]{2,1,0:T(8,128)(2,1)S(1)}, u32[]{:S(2)}, u32[]{:S(2)}) collective-permute-start(bf16[1,64,320]{2,1,0:T(8,128)(2,1)S(1)} %get-tuple-element.80), channel_id=1, source_target_pairs={{32,0},{64,32},{96,64},{128,96},{160,128},{192,160},{224,192},{256... | collective-permute-start | bytes 122888 | tf_op jit(solution)/shard_map/ppermute | solution.py:20
  115.2 6.8 %collective-permute-start.14 = (bf16[14,1,320]{2,1,0:T(2,128)(2,1)S(1)}, bf16[14,1,320]{2,1,0:T(2,128)(2,1)S(1)}, u32[]{:S(2)}, u32[]{:S(2)}) collective-permute-start(bf16[14,1,320]{2,1,0:T(2,128)(2,1)S(1)} %get-tuple-element.59), channel_id=1, source_target_pairs={{0,2},{2,4},{4,6},{6,8},{8,10},{10,12},{12,14},{14,16},{16,18},{18... | collective-permute-start | bytes 26888 | tf_op jit(solution)/shard_map/ppermute | solution.py:17
  118.4 6.3 %collective-permute-start.15 = (bf16[14,1,320]{2,1,0:T(2,128)(2,1)S(1)}, bf16[14,1,320]{2,1,0:T(2,128)(2,1)S(1)}, u32[]{:S(2)}, u32[]{:S(2)}) collective-permute-start(bf16[14,1,320]{2,1,0:T(2,128)(2,1)S(1)} %get-tuple-element.60), channel_id=1, source_target_pairs={{2,0},{4,2},{6,4},{8,6},{10,8},{12,10},{14,12},{16,14},{18,16},{20... | collective-permute-start | bytes 26888 | tf_op jit(solution)/shard_map/ppermute | solution.py:20
  138.4 14.3 %copy-start.4 = (bf16[9,320,4]{1,2,0:T(4,128)(2,1)S(1)}, bf16[9,320,4]{1,2,0:T(4,128)(2,1)}, u32[]{:S(2)}) copy-start(bf16[9,320,4]{1,2,0:T(4,128)(2,1)} %param.23) | copy-start | bytes 69124
  138.4 5.4 %collective-permute-start.16 = (bf16[1,64,320]{2,1,0:T(8,128)(2,1)S(1)}, bf16[1,64,320]{2,1,0:T(8,128)(2,1)S(1)}, u32[]{:S(2)}, u32[]{:S(2)}) collective-permute-start(bf16[1,64,320]{2,1,0:T(8,128)(2,1)S(1)} %get-tuple-element.75), channel_id=1, source_target_pairs={{0,32},{32,64},{64,96},{96,128},{128,160},{160,192},{192,224},{224... | collective-permute-start | bytes 122888 | tf_op jit(solution)/shard_map/ppermute | solution.py:17
  140.4 6.9 %collective-permute-start.17 = (bf16[1,64,320]{2,1,0:T(8,128)(2,1)S(1)}, bf16[1,64,320]{2,1,0:T(8,128)(2,1)S(1)}, u32[]{:S(2)}, u32[]{:S(2)}) collective-permute-start(bf16[1,64,320]{2,1,0:T(8,128)(2,1)S(1)} %get-tuple-element.76), channel_id=1, source_target_pairs={{32,0},{64,32},{96,64},{128,96},{160,128},{192,160},{224,192},{256... | collective-permute-start | bytes 122888 | tf_op jit(solution)/shard_map/ppermute | solution.py:20
  147.3 5.6 %collective-permute-start.18 = (bf16[14,1,320]{2,1,0:T(2,128)(2,1)S(1)}, bf16[14,1,320]{2,1,0:T(2,128)(2,1)S(1)}, u32[]{:S(2)}, u32[]{:S(2)}) collective-permute-start(bf16[14,1,320]{2,1,0:T(2,128)(2,1)S(1)} %get-tuple-element.55), channel_id=1, source_target_pairs={{0,2},{2,4},{4,6},{6,8},{8,10},{10,12},{12,14},{14,16},{16,18},{18... | collective-permute-start | bytes 26888 | tf_op jit(solution)/shard_map/ppermute | solution.py:17
  150.6 6.3 %collective-permute-start.19 = (bf16[14,1,320]{2,1,0:T(2,128)(2,1)S(1)}, bf16[14,1,320]{2,1,0:T(2,128)(2,1)S(1)}, u32[]{:S(2)}, u32[]{:S(2)}) collective-permute-start(bf16[14,1,320]{2,1,0:T(2,128)(2,1)S(1)} %get-tuple-element.56), channel_id=1, source_target_pairs={{2,0},{4,2},{6,4},{8,6},{10,8},{12,10},{14,12},{16,14},{18,16},{20... | collective-permute-start | bytes 26888 | tf_op jit(solution)/shard_map/ppermute | solution.py:20
  157.9 1.0 copy-start.3
  159.6 1.2 copy-start.8
  159.6 14.5 %copy-start.5 = (f32[2,12,64]{2,0,1:T(2,128)S(1)}, f32[2,12,64]{2,0,1:T(2,128)}, u32[]{:S(2)}) copy-start(f32[2,12,64]{2,0,1:T(2,128)} %param.15) | copy-start | bytes 18436
  160.9 13.2 %collective-permute-start.20 = (f32[2,12,64]{2,1,0:T(8,128)S(1)}, f32[2,12,64]{2,1,0:T(8,128)S(1)}, u32[]{:S(2)}, u32[]{:S(2)}) collective-permute-start(f32[2,12,64]{2,1,0:T(8,128)S(1)} %dynamic-slice_bitcast_fusion), channel_id=1, source_target_pairs={{0,1},{1,0},{2,3},{3,2},{4,5},{5,4},{6,7},{7,6},{8,9},{9,8},{10,11... | collective-permute-start | bytes 18440 | tf_op jit(solution)/shard_map/ppermute | solution.py:28
where the time goes:
time: 178 us; the launch traced here: 176 us
  starting transfers between devices  66.9 us (38%)
  matrix products  55.9 us (31%)
  waiting for transfers between devices  32.2 us (18%)
  local copies, waits for them, and re-layouts  9.85 us (6%)
  other arithmetic  8.93 us (5%)
  between operations  2.21 us (1%)
    dot_general x45, matrix products, conv_valid(): jnp.dot(window, kernel[tap_index], preferred_element_type=jnp.float32)  55.9 us
    ppermute x10, starting transfers between devices, extended(): lax.ppermute(lax.slice_in_dim(block, block.shape[dim] - width, None, axis...  30.7 us
    ppermute x10, waiting for transfers between devices, extended(): lax.ppermute(lax.slice_in_dim(block, 0, width, axis=dim), axis, backward)  30.6 us
    ppermute x10, starting transfers between devices, extended(): lax.ppermute(lax.slice_in_dim(block, 0, width, axis=dim), axis, backward)  25.7 us
    ppermute x1, starting transfers between devices, partner_2(): return lax.ppermute(value, axis, pairs)  10.4 us
  transfers between devices with their start and end apart: 21, of which 11 were waited for; matrix products, arithmetic and copies ran while one was open for 5% of the time, Pallas kernels for 0%

commit v1 on v0

v1 whole, which is shorter than its diff:
```python
import jax
import jax.numpy as jnp
from jax import lax
from jax.experimental import pallas as pl
from jax.experimental.pallas import tpu as pltpu
from jax.sharding import PartitionSpec as P

MESH = pl.DeviceIdType.MESH
BF, F32 = jnp.bfloat16, jnp.float32

C = 320
GROUPS = 32
ROWS, COLS = 12, 64
HALO = 5
WIDE = COLS + 2 * HALO
TALL = ROWS + 2 * HALO
STRIP = 16
STAGE = COLS + 2 * STRIP
STEP = WIDE + 1
TILE = 256
TILES = (6, 6, 5, 5)
GRID_ROWS, GRID_COLS = 16, 16
NORM_EPS = 1e-05

A_COL, B_COL, BIAS_COL = 0, 5, 10


def exact_parts(value):
    high = value.astype(BF).astype(F32)
    mid = (value - high).astype(BF).astype(F32)
    return high, mid, value - high - mid


def kernel(
    features,
    weight,
    latent,
    bias,
    gain,
    shift,
    emb,
    mean,
    var,
    out_weight,
    out_bias,
    guidance,
    timestep,
    coeffs,
    out,
    stage,
    wraw,
    wflat,
    patches,
    act_a,
    act_b,
    hid_a,
    hid_b,
    params,
    pcols,
    masks,
    wout,
    taps,
    eps,
    partner,
    load_sem,
    wsem,
    send_sem,
    recv_sem,
    cfg_send,
    cfg_recv,
):
    row, col, cfg = lax.axis_index("row"), lax.axis_index("col"), lax.axis_index("cfg")
    has = {
        (-1, 0): row > 0,
        (1, 0): row < GRID_ROWS - 1,
        (0, -1): col > 0,
        (0, 1): col < GRID_COLS - 1,
    }
    for dr in (-1, 1):
        for dc in (-1, 1):
            has[dr, dc] = has[dr, 0] & has[0, dc]
    sides = list(has)

    edge = (row == 0) | (row == GRID_ROWS - 1) | (col == 0) | (col == GRID_COLS - 1)

    @pl.when(edge)
    def _():
        stage[...] = jnp.zeros_like(stage)

    barrier = pltpu.get_barrier_semaphore()
    for dr, dc in sides:

        @pl.when(has[dr, dc])
        def _(dr=dr, dc=dc):
            pl.semaphore_signal(
                barrier, inc=1, device_id={"row": row + dr, "col": col + dc}, device_id_type=MESH
            )

    pl.semaphore_signal(barrier, inc=1, device_id={"cfg": 1 - cfg}, device_id_type=MESH)

    own = pltpu.make_async_copy(
        features.at[0], stage.at[pl.ds(HALO, ROWS), pl.ds(STRIP, COLS)], load_sem
    )
    own.start()
    loads = []
    for n in range(4):
        load = pltpu.make_async_copy(weight.at[n // 2, n % 2], wraw.at[n], wsem.at[n])
        load.start()
        loads.append(load)

    groups = lax.broadcasted_iota(jnp.int32, (GROUPS, C), 0)
    channels = lax.broadcasted_iota(jnp.int32, (GROUPS, C), 1)
    lowest = groups * (C // GROUPS)
    spread = jnp.where((channels >= lowest) & (channels < lowest + C // GROUPS), 1.0, 0.0).astype(F32)

    def to_channels(value):
        total = None
        for part in exact_parts(value):
            term = jnp.dot(part, spread, preferred_element_type=F32)
            total = term if total is None else total + term
        return total

    scale = to_channels(lax.rsqrt(var[0] + NORM_EPS)) * gain[...]
    offset = shift[...] - to_channels(mean[0]) * scale
    params[...] = jnp.zeros_like(params)
    for n in range(5):
        add = offset[n : n + 1]
        if n in (1, 3):
            k = n // 2
            add = add + scale[n : n + 1] * (bias[k, 0:1] + emb[0, k : k + 1])
        params[A_COL + n : A_COL + n + 1, 0:C] = 0.5 * scale[n : n + 1]
        params[B_COL + n : B_COL + n + 1, 0:C] = 0.5 * add
    for k in range(2):
        params[BIAS_COL + k : BIAS_COL + k + 1, 0:C] = bias[k, 1:2]
    pcols[...] = jnp.transpose(params[...])

    for t in range(9):
        padded = jnp.concatenate([out_weight[t].astype(F32), jnp.zeros((C, 4), F32)], axis=1)
        wout[8 * t : 8 * t + 8, :] = jnp.transpose(padded)

    for n in range(5):
        cell = lax.broadcasted_iota(jnp.int32, (8, masks.shape[2]), 1) + n * STEP
        cell_row = lax.shift_right_logical(cell * 28340, 21)
        cell_col = cell - cell_row * WIDE
        grid_row = cell_row + (row * ROWS - HALO)
        grid_col = cell_col + (col * COLS - HALO)
        inside = (
            (grid_row >= 0)
            & (grid_row < GRID_ROWS * ROWS)
            & (grid_col >= 0)
            & (grid_col < GRID_COLS * COLS)
        )
        masks[n] = jnp.where(inside, 1.0, 0.0).astype(F32)

    eye_row = lax.broadcasted_iota(jnp.int32, (C, C), 0)
    eye_col = lax.broadcasted_iota(jnp.int32, (C, C), 1)
    eye = jnp.where(eye_row == eye_col, 1.0, 0.0).astype(BF)

    def flipped(value):
        return lax.dot_general(
            eye, value, (((1,), (1,)), ((), ())), preferred_element_type=F32
        ).astype(BF)

    arrivals = sum(jnp.where(has[s], 1, 0) for s in sides) + 1
    pl.semaphore_wait(barrier, arrivals)

    row_src = {-1: pl.ds(0, HALO), 0: pl.ds(0, ROWS), 1: pl.ds(ROWS - HALO, HALO)}
    row_dst = {-1: pl.ds(HALO + ROWS, HALO), 0: pl.ds(HALO, ROWS), 1: pl.ds(0, HALO)}
    col_src = {-1: pl.ds(0, STRIP), 0: pl.ds(0, COLS), 1: pl.ds(COLS - STRIP, STRIP)}
    col_dst = {-1: pl.ds(STRIP + COLS, STRIP), 0: pl.ds(STRIP, COLS), 1: pl.ds(0, STRIP)}
    copies = {}
    for n, (dr, dc) in enumerate(sides):
        copy = pltpu.make_async_remote_copy(
            src_ref=features.at[0, row_src[dr], col_src[dc]],
            dst_ref=stage.at[row_dst[dr], col_dst[dc]],
            send_sem=send_sem.at[n],
            recv_sem=recv_sem.at[n],
            device_id={"row": row + dr, "col": col + dc},
            device_id_type=MESH,
        )
        copies[dr, dc] = copy

        @pl.when(has[dr, dc])
        def _(copy=copy):
            copy.start()

    for n in range(4):
        loads[n].wait()

        @pl.loop(0, 1)
        def _(_, n=n):
            wflat[n] = flipped(wraw[n].reshape(9 * C, C))

    own.wait()
    for dr, dc in sides:
        copy = copies[dr, dc]

        @pl.when(has[-dr, -dc])
        def _(copy=copy):
            copy.wait_recv()

    def silu(values, norm, frame, first):
        size = values.shape[1]
        half = values * pcols[0:C, A_COL + norm : A_COL + norm + 1] + pcols[
            0:C, B_COL + norm : B_COL + norm + 1
        ]
        masked = half * masks[frame, 0:1, first : first + size]
        return (masked * (1.0 + jnp.tanh(half))).astype(BF)

    for first, count in ((HALO, ROWS), (0, HALO), (HALO + ROWS, HALO)):
        turned = flipped(stage[first : first + count].reshape(count * STAGE, C))
        for n in range(count):
            begin = n * STAGE + STRIP - HALO
            hid_a[:, (first + n) * WIDE : (first + n + 1) * WIDE] = turned[:, begin : begin + WIDE]
    hid_a[:, TALL * WIDE :] = jnp.zeros((C, hid_a.shape[1] - TALL * WIDE), BF)
    for n in range(hid_a.shape[1] // TILE):
        part = slice(n * TILE, (n + 1) * TILE)
        act_a[:, part] = silu(hid_a[:, part].astype(F32), 0, 0, n * TILE)

    def conv(layer, source, finish):
        size = TILES[layer] * TILE
        for p in range(3):
            for q in range(3):
                tap = 3 * p + q
                patches[tap * C : (tap + 1) * C, 0:size] = source[:, p * WIDE + q : p * WIDE + q + size]
        for n in range(TILES[layer]):
            part = slice(n * TILE, (n + 1) * TILE)
            finish(part, jnp.dot(wflat[layer], patches[:, part], preferred_element_type=F32))

    def inner(layer, dest):
        def finish(part, total):
            dest[:, part] = silu(total, layer + 1, layer + 1, part.start)

        return finish

    def outer(layer, before, after, dest):
        k = layer // 2

        def finish(part, total):
            skip = before[:, part.start + 2 * STEP : part.stop + 2 * STEP].astype(F32)
            hidden = (skip + (total + pcols[0:C, BIAS_COL + k : BIAS_COL + k + 1])).astype(BF)
            if after is not None:
                after[:, part] = hidden
            dest[:, part] = silu(hidden.astype(F32), layer + 1, layer + 1, part.start)

        return finish

    conv(0, act_a, inner(0, act_b))
    conv(1, act_b, outer(1, hid_a, hid_b, act_a))
    conv(2, act_a, inner(2, act_b))
    conv(3, act_b, outer(3, hid_b, None, act_a))

    size = eps.shape[2]
    taps[...] = jnp.dot(wout[...].astype(BF), act_a[:, 0 : taps.shape[1]], preferred_element_type=F32)
    total = None
    for p in range(3):
        for q in range(3):
            t = 3 * p + q
            begin = p * WIDE + q
            term = taps[8 * t : 8 * t + 8, begin : begin + size]
            total = term if total is None else total + term
    for o in range(4):
        eps[o // 2, o % 2 : o % 2 + 1, :] = total[o : o + 1] + out_bias[o]

    swap = pltpu.make_async_remote_copy(
        src_ref=eps.at[1 - cfg],
        dst_ref=partner,
        send_sem=cfg_send,
        recv_sem=cfg_recv,
        device_id={"cfg": 1 - cfg},
        device_id_type=MESH,
    )
    swap.start()
    for dr, dc in sides:
        copy = copies[dr, dc]

        @pl.when(has[dr, dc])
        def _(copy=copy):
            copy.wait_send()

    swap.wait()
    mine, other = eps[cfg], partner[...]
    uncond = jnp.where(cfg == 1, other, mine)
    cond = jnp.where(cfg == 1, mine, other)
    guided = uncond + guidance[0] * (cond - uncond)
    step = timestep[0]
    c_latent, c_guided = coeffs[step, 0], coeffs[step, 1]
    for n in range(ROWS):
        out[:, n, :] = c_latent * latent[:, n, :] + c_guided * guided[:, n * WIDE : n * WIDE + COLS]


def per_device(
    features,
    latent,
    conv_weight,
    conv_bias,
    norm_gain,
    norm_shift,
    emb_shift,
    stale_mean,
    stale_var,
    out_weight,
    out_bias,
    guidance,
    timestep,
    coeffs,
):
    hbm = pl.BlockSpec(memory_space=pl.ANY)
    vmem = pl.BlockSpec(memory_space=pltpu.VMEM)
    smem = pl.BlockSpec(memory_space=pltpu.SMEM)
    dma = pltpu.SemaphoreType.DMA
    lanes = 1792
    return pl.pallas_call(
        kernel,
        out_shape=jax.ShapeDtypeStruct(latent.shape, F32),
        in_specs=[hbm, hbm] + [vmem] * 8 + [smem] * 4,
        out_specs=vmem,
        scratch_shapes=[
            pltpu.VMEM((TALL, STAGE, C), BF),
            pltpu.VMEM((4, 9, C, C), BF),
            pltpu.VMEM((4, C, 9 * C), BF),
            pltpu.VMEM((9 * C, TILES[0] * TILE), BF),
            pltpu.VMEM((C, lanes), BF),
            pltpu.VMEM((C, lanes), BF),
            pltpu.VMEM((C, lanes), BF),
            pltpu.VMEM((C, lanes), BF),
            pltpu.VMEM((128, 384), F32),
            pltpu.VMEM((384, 128), F32),
            pltpu.VMEM((5, 8, lanes), F32),
            pltpu.VMEM((72, C), F32),
            pltpu.VMEM((72, 1152), F32),
            pltpu.VMEM((2, 2, 896), F32),
            pltpu.VMEM((2, 896), F32),
            dma,
            dma((4,)),
            dma((8,)),
            dma((8,)),
            dma,
            dma,
        ],
        compiler_params=pltpu.CompilerParams(
            collective_id=0, has_side_effects=True, vmem_limit_bytes=58 * 2**20
        ),
        cost_estimate=pl.CostEstimate(
            flops=12 * 10**9, bytes_accessed=10 * 2**20, transcendentals=2 * 10**6
        ),
    )(
        features,
        conv_weight,
        latent,
        conv_bias,
        norm_gain,
        norm_shift,
        emb_shift,
        stale_mean,
        stale_var,
        out_weight,
        out_bias,
        guidance,
        timestep,
        coeffs,
    )


def solution(mesh):
    return jax.shard_map(
        per_device,
        mesh=mesh,
        in_specs=(
            P("cfg", "row", "col", None),
            P("cfg", "row", "col"),
            P(),
            P(),
            P(),
            P(),
            P("cfg", None, None),
            P("cfg", None, None),
            P("cfg", None, None),
            P(),
            P(),
            P(),
            P(),
            P(),
        ),
        out_specs=P("cfg", "row", "col"),
        check_vma=False,
    )
```

time: 178 us -> 64.6 us (0.36)
  the two profiles are of different devices: /device:TPU:123 before, /device:TPU:6 now
where the time goes in v1:
time: 64.6 us; the launch traced here: 64.2 us
  Pallas kernels  54.3 us (84%)
  local copies, waits for them, and re-layouts  8.51 us (13%)
  between operations  1.31 us (2%)
    pallas_call x1, Pallas kernels, per_device(): pl.pallas_call(kernel, out_shape=jax.ShapeDtypeStruct(latent.shape, F32),...  54.3 us
    unnamed x5, local copies, waits for them, and re-layouts  7.18 us
    pallas_call x1, local copies, waits for them, and re-layouts, per_device(): pl.pallas_call(kernel, out_shape=jax.ShapeDtypeStruct(latent.shape, F32),...  1.32 us

profile of v1, /device:TPU:6, one launch (start us, length us, event | category | flops | bytes accessed | tf_op | source)
XLA Modules:
  0.0 64.2 jit_solution(1771927346958140642)
XLA Ops:
  1.3 1.3 %copy.16.mean = f32[1,5,32]{2,1,0:T(8,128)} copy(f32[1,5,32]{2,0,1:T(1,128)} %param.21) | data formatting | bytes 1280 | tf_op args[7]
  2.6 1.3 %copy.17.var = f32[1,5,32]{2,1,0:T(8,128)} copy(f32[1,5,32]{2,0,1:T(1,128)} %param.22) | data formatting | bytes 1280 | tf_op args[8]
  3.8 1.3 %copy.15.latent = f32[2,12,64]{2,1,0:T(8,128)} copy(f32[2,12,64]{2,0,1:T(2,128)} %param.15) | data formatting | bytes 12288 | tf_op args[1]
  5.2 1.4 %copy.19.coeffs = f32[50,2]{1,0:T(8,128)} copy(f32[50,2]{0,1:T(2,128)} %param.27) | data formatting | bytes 800 | tf_op args[13]
  6.5 1.9 %copy.18.out_weight = bf16[9,320,4]{2,1,0:T(8,128)(2,1)} copy(bf16[9,320,4]{1,2,0:T(4,128)(2,1)} %param.23) | data formatting | bytes 46080 | tf_op args[9]
  8.5 54.3 %shard_map.136 = f32[2,12,64]{2,1,0:T(8,128)} custom-call(bf16[1,12,64,320]{3,2,1,0:T(8,128)(2,1)} %features.1, bf16[2,2,9,320,320]{4,3,2,1,0:T(8,128)(2,1)} %weight.1, f32[2,12,64]{2,1,0:T(8,128)} %copy.15.latent, f32[2,2,320]{2,1,0:T(2,128)} %bias.1, f32[5,320]{1,0:T(8,128)} %gain.1, f32[5,320]{1,0:T(8,128)} %shift.1, f32[1,2,320]{2,1,0:T(2,128)} %emb.1, ...), custom_call_target="tpu_custom_call" | custom-call | flops 12000000000 | bytes 10485760 | tf_op jit(solution)/shard_map/pallas_call | solution.py:313
  62.8 1.3 %copy.20 = f32[2,12,64]{2,0,1:T(2,128)} copy(f32[2,12,64]{2,1,0:T(8,128)} %shard_map.136) | data formatting | bytes 12288 | tf_op jit(solution)/shard_map/pallas_call | solution.py:313

commit v2 on v1

--- a/solution.py
+++ b/solution.py
@@ -18,6 +18,7 @@
 STAGE = COLS + 2 * STRIP
 STEP = WIDE + 1
 TILE = 256
+LANES = 128
 TILES = (6, 6, 5, 5)
 GRID_ROWS, GRID_COLS = 16, 16
 NORM_EPS = 1e-05
@@ -55,6 +56,7 @@
     act_b,
     hid_a,
     hid_b,
+    hid_s,
     params,
     pcols,
     masks,
@@ -120,8 +122,8 @@
             total = term if total is None else total + term
         return total
 
-    scale = to_channels(lax.rsqrt(var[0] + NORM_EPS)) * gain[...]
-    offset = shift[...] - to_channels(mean[0]) * scale
+    scale = to_channels(lax.rsqrt(var[:, 0, :] + NORM_EPS)) * gain[...]
+    offset = shift[...] - to_channels(mean[:, 0, :]) * scale
     params[...] = jnp.zeros_like(params)
     for n in range(5):
         add = offset[n : n + 1]
@@ -132,11 +134,13 @@
         params[B_COL + n : B_COL + n + 1, 0:C] = 0.5 * add
     for k in range(2):
         params[BIAS_COL + k : BIAS_COL + k + 1, 0:C] = bias[k, 1:2]
-    pcols[...] = jnp.transpose(params[...])
-
+    turned_params = jnp.transpose(params[...])
+    for n in range(12):
+        pcols[n] = jnp.broadcast_to(turned_params[0:C, n : n + 1], (C, LANES))
+
+    wout[...] = jnp.zeros_like(wout)
     for t in range(9):
-        padded = jnp.concatenate([out_weight[t].astype(F32), jnp.zeros((C, 4), F32)], axis=1)
-        wout[8 * t : 8 * t + 8, :] = jnp.transpose(padded)
+        wout[8 * t : 8 * t + 4, :] = out_weight[t].astype(F32)
 
     for n in range(5):
         cell = lax.broadcasted_iota(jnp.int32, (8, masks.shape[2]), 1) + n * STEP
@@ -199,13 +203,13 @@
         def _(copy=copy):
             copy.wait_recv()
 
-    def silu(values, norm, frame, first):
-        size = values.shape[1]
-        half = values * pcols[0:C, A_COL + norm : A_COL + norm + 1] + pcols[
-            0:C, B_COL + norm : B_COL + norm + 1
-        ]
-        masked = half * masks[frame, 0:1, first : first + size]
-        return (masked * (1.0 + jnp.tanh(half))).astype(BF)
+    def silu(dest, values, norm, frame, first):
+        for n in range(values.shape[1] // LANES):
+            part = slice(n * LANES, (n + 1) * LANES)
+            place = slice(first + n * LANES, first + (n + 1) * LANES)
+            half = values[:, part] * pcols[A_COL + norm] + pcols[B_COL + norm]
+            masked = half * masks[frame, 0:1, place]
+            dest[:, place] = (masked * (1.0 + jnp.tanh(half))).astype(BF)
 
     for first, count in ((HALO, ROWS), (0, HALO), (HALO + ROWS, HALO)):
         turned = flipped(stage[first : first + count].reshape(count * STAGE, C))
@@ -215,7 +219,7 @@
     hid_a[:, TALL * WIDE :] = jnp.zeros((C, hid_a.shape[1] - TALL * WIDE), BF)
     for n in range(hid_a.shape[1] // TILE):
         part = slice(n * TILE, (n + 1) * TILE)
-        act_a[:, part] = silu(hid_a[:, part].astype(F32), 0, 0, n * TILE)
+        silu(act_a, hid_a[:, part].astype(F32), 0, 0, n * TILE)
 
     def conv(layer, source, finish):
         size = TILES[layer] * TILE
@@ -229,7 +233,7 @@
 
     def inner(layer, dest):
         def finish(part, total):
-            dest[:, part] = silu(total, layer + 1, layer + 1, part.start)
+            silu(dest, total, layer + 1, layer + 1, part.start)
 
         return finish
 
@@ -237,18 +241,27 @@
         k = layer // 2
 
         def finish(part, total):
-            skip = before[:, part.start + 2 * STEP : part.stop + 2 * STEP].astype(F32)
-            hidden = (skip + (total + pcols[0:C, BIAS_COL + k : BIAS_COL + k + 1])).astype(BF)
-            if after is not None:
-                after[:, part] = hidden
-            dest[:, part] = silu(hidden.astype(F32), layer + 1, layer + 1, part.start)
+            for n in range(TILE // LANES):
+                place = slice(part.start + n * LANES, part.start + (n + 1) * LANES)
+                skip = before[:, place].astype(F32)
+                inc = total[:, n * LANES : (n + 1) * LANES] + pcols[BIAS_COL + k]
+                hidden = (skip + inc).astype(BF)
+                if after is not None:
+                    after[:, place] = hidden
+                silu(dest, hidden.astype(F32), layer + 1, layer + 1, place.start)
 
         return finish
 
+    def shifted(dest, source, layer):
+        size = TILES[layer] * TILE
+        dest[:, 0:size] = source[:, 2 * STEP : 2 * STEP + size]
+
+    shifted(hid_s, hid_a, 1)
     conv(0, act_a, inner(0, act_b))
-    conv(1, act_b, outer(1, hid_a, hid_b, act_a))
+    conv(1, act_b, outer(1, hid_s, hid_b, act_a))
     conv(2, act_a, inner(2, act_b))
-    conv(3, act_b, outer(3, hid_b, None, act_a))
+    shifted(hid_s, hid_b, 3)
+    conv(3, act_b, outer(3, hid_s, None, act_a))
 
     size = eps.shape[2]
     taps[...] = jnp.dot(wout[...].astype(BF), act_a[:, 0 : taps.shape[1]], preferred_element_type=F32)
@@ -284,9 +297,9 @@
     cond = jnp.where(cfg == 1, mine, other)
     guided = uncond + guidance[0] * (cond - uncond)
     step = timestep[0]
-    c_latent, c_guided = coeffs[step, 0], coeffs[step, 1]
+    c_latent, c_guided = coeffs[0, step], coeffs[1, step]
     for n in range(ROWS):
-        out[:, n, :] = c_latent * latent[:, n, :] + c_guided * guided[:, n * WIDE : n * WIDE + COLS]
+        out[n] = c_latent * latent[n] + c_guided * guided[:, n * WIDE : n * WIDE + COLS]
 
 
 def per_device(
@@ -310,9 +323,12 @@
     smem = pl.BlockSpec(memory_space=pltpu.SMEM)
     dma = pltpu.SemaphoreType.DMA
     lanes = 1792
-    return pl.pallas_call(
+    def swapped(value):
+        return jnp.transpose(value, (1, 0, 2))
+
+    result = pl.pallas_call(
         kernel,
-        out_shape=jax.ShapeDtypeStruct(latent.shape, F32),
+        out_shape=jax.ShapeDtypeStruct((ROWS, 2, COLS), F32),
         in_specs=[hbm, hbm] + [vmem] * 8 + [smem] * 4,
         out_specs=vmem,
         scratch_shapes=[
@@ -324,8 +340,9 @@
             pltpu.VMEM((C, lanes), BF),
             pltpu.VMEM((C, lanes), BF),
             pltpu.VMEM((C, lanes), BF),
+            pltpu.VMEM((C, lanes), BF),
             pltpu.VMEM((128, 384), F32),
-            pltpu.VMEM((384, 128), F32),
+            pltpu.VMEM((12, C, LANES), F32),
             pltpu.VMEM((5, 8, lanes), F32),
             pltpu.VMEM((72, C), F32),
             pltpu.VMEM((72, 1152), F32),
@@ -347,19 +364,20 @@
     )(
         features,
         conv_weight,
-        latent,
+        swapped(latent),
         conv_bias,
         norm_gain,
         norm_shift,
         emb_shift,
-        stale_mean,
-        stale_var,
-        out_weight,
+        swapped(stale_mean),
+        swapped(stale_var),
+        jnp.transpose(out_weight, (0, 2, 1)),
         out_bias,
         guidance,
         timestep,
-        coeffs,
+        jnp.transpose(coeffs),
     )
+    return swapped(result)
 
 
 def solution(mesh):

time: 64.6 us -> 49.1 us (0.76)
  Pallas kernels: 54.3 us -> 46 us
  local copies, waits for them, and re-layouts: 8.51 us -> 1.31 us
    pallas_call x1, Pallas kernels: 54.3 us -> 46 us  [per_device(): pl.pallas_call(kernel, out_shape=jax.ShapeDtypeStruct((ROWS, 2, COLS), F3...]
    unnamed x5 -> x1, local copies, waits for them, and re-layouts: 7.18 us -> 1.31 us
    pallas_call x1 -> x0, local copies, waits for them, and re-layouts: 1.32 us -> none  [per_device(): pl.pallas_call(kernel, out_shape=jax.ShapeDtypeStruct(latent.shape, F32),...]
where the time goes in v2:
time: 49.1 us; the launch traced here: 48.6 us
  Pallas kernels  46 us (94%)
  local copies, waits for them, and re-layouts  1.31 us (3%)
  between operations  1.31 us (3%)
    pallas_call x1, Pallas kernels, per_device(): pl.pallas_call(kernel, out_shape=jax.ShapeDtypeStruct((ROWS, 2, COLS), F3...  46 us
    unnamed x1, local copies, waits for them, and re-layouts  1.31 us

profile of v2, /device:TPU:6, one launch (start us, length us, event | category | flops | bytes accessed | tf_op | source)
XLA Modules:
  0.0 48.6 jit_solution(6814733535517969175)
XLA Ops:
  1.3 46.0 %shard_map.136 = f32[12,2,64]{2,1,0:T(2,128)} custom-call(bf16[1,12,64,320]{3,2,1,0:T(8,128)(2,1)} %features.1, bf16[2,2,9,320,320]{4,3,2,1,0:T(8,128)(2,1)} %weight.1, f32[12,2,64]{2,1,0:T(2,128)} %bitcast.8, f32[2,2,320]{2,1,0:T(2,128)} %bias.1, f32[5,320]{1,0:T(8,128)} %gain.1, f32[5,320]{1,0:T(8,128)} %shift.1, f32[1,2,320]{2,1,0:T(2,128)} %emb.1, ...), custom_call_target="tpu_custom_call" | custom-call | flops 12000000000 | bytes 10485760 | tf_op jit(solution)/shard_map/pallas_call | solution.py:329
  47.3 1.3 %copy.18 = f32[2,12,64]{2,0,1:T(2,128)} copy(f32[2,12,64]{2,0,1:T(2,128)} %bitcast.6) | data formatting | bytes 12288

commit v3 on v2

--- a/solution.py
+++ b/solution.py
@@ -14,8 +14,11 @@
 HALO = 5
 WIDE = COLS + 2 * HALO
 TALL = ROWS + 2 * HALO
-STRIP = 16
-STAGE = COLS + 2 * STRIP
+STRIP = 8
+LEFT = 16
+STAGE = COLS + 2 * LEFT
+CORNER = 6 * STRIP
+PARTS = (((HALO, ROWS, 0),), ((0, HALO, -1), (HALO + ROWS, HALO, 1)))
 STEP = WIDE + 1
 TILE = 256
 LANES = 128
@@ -35,6 +38,28 @@
 def kernel(
     features,
     weight,
+    guidance_in,
+    timestep_in,
+    coeffs_in,
+    out_bias_in,
+    latent_in,
+    bias_in,
+    gain_in,
+    shift_in,
+    emb_in,
+    mean_in,
+    var_in,
+    out_weight_in,
+    out,
+    stage_own,
+    stage_halo,
+    strips,
+    sides_in,
+    corners_in,
+    guidance,
+    timestep,
+    coeffs,
+    out_bias,
     latent,
     bias,
     gain,
@@ -43,12 +68,7 @@
     mean,
     var,
     out_weight,
-    out_bias,
-    guidance,
-    timestep,
-    coeffs,
-    out,
-    stage,
+    small_sem,
     wraw,
     wflat,
     patches,
@@ -87,7 +107,8 @@
 
     @pl.when(edge)
     def _():
-        stage[...] = jnp.zeros_like(stage)
+        for ref in (stage_halo, sides_in, corners_in):
+            ref[...] = jnp.zeros_like(ref)
 
     barrier = pltpu.get_barrier_semaphore()
     for dr, dc in sides:
@@ -101,15 +122,38 @@
     pl.semaphore_signal(barrier, inc=1, device_id={"cfg": 1 - cfg}, device_id_type=MESH)
 
     own = pltpu.make_async_copy(
-        features.at[0], stage.at[pl.ds(HALO, ROWS), pl.ds(STRIP, COLS)], load_sem
+        features.at[0], stage_own.at[:, pl.ds(LEFT, COLS)], load_sem
     )
     own.start()
+    small = []
+    for n, (source, dest) in enumerate(
+        (
+            (gain_in, gain),
+            (shift_in, shift),
+            (mean_in, mean),
+            (var_in, var),
+            (bias_in, bias),
+            (emb_in, emb),
+            (out_weight_in, out_weight),
+            (latent_in, latent),
+            (guidance_in, guidance),
+            (timestep_in, timestep),
+            (coeffs_in, coeffs),
+            (out_bias_in, out_bias),
+        )
+    ):
+        load = pltpu.make_async_copy(source, dest, small_sem.at[n])
+        load.start()
+        small.append(load)
+    early, small = small[:7], small[7:]
     loads = []
     for n in range(4):
         load = pltpu.make_async_copy(weight.at[n // 2, n % 2], wraw.at[n], wsem.at[n])
         load.start()
         loads.append(load)
 
+    for load in early:
+        load.wait()
     groups = lax.broadcasted_iota(jnp.int32, (GROUPS, C), 0)
     channels = lax.broadcasted_iota(jnp.int32, (GROUPS, C), 1)
     lowest = groups * (C // GROUPS)
@@ -165,28 +209,64 @@
             eye, value, (((1,), (1,)), ((), ())), preferred_element_type=F32
         ).astype(BF)
 
+    own.wait()
+    for n in range(ROWS):
+        cells = slice(n * STRIP, (n + 1) * STRIP)
+        strips[0, cells] = stage_own[n, LEFT : LEFT + STRIP]
+        strips[1, cells] = stage_own[n, LEFT + COLS - STRIP : LEFT + COLS]
+
     arrivals = sum(jnp.where(has[s], 1, 0) for s in sides) + 1
     pl.semaphore_wait(barrier, arrivals)
 
-    row_src = {-1: pl.ds(0, HALO), 0: pl.ds(0, ROWS), 1: pl.ds(ROWS - HALO, HALO)}
-    row_dst = {-1: pl.ds(HALO + ROWS, HALO), 0: pl.ds(HALO, ROWS), 1: pl.ds(0, HALO)}
-    col_src = {-1: pl.ds(0, STRIP), 0: pl.ds(0, COLS), 1: pl.ds(COLS - STRIP, STRIP)}
-    col_dst = {-1: pl.ds(STRIP + COLS, STRIP), 0: pl.ds(STRIP, COLS), 1: pl.ds(0, STRIP)}
-    copies = {}
-    for n, (dr, dc) in enumerate(sides):
+    copies = []
+
+    def send(dr, dc, source, dest):
+        n = len(copies)
         copy = pltpu.make_async_remote_copy(
-            src_ref=features.at[0, row_src[dr], col_src[dc]],
-            dst_ref=stage.at[row_dst[dr], col_dst[dc]],
+            src_ref=source,
+            dst_ref=dest,
             send_sem=send_sem.at[n],
             recv_sem=recv_sem.at[n],
             device_id={"row": row + dr, "col": col + dc},
             device_id_type=MESH,
         )
-        copies[dr, dc] = copy
+        copies.append((copy, has[dr, dc], has[-dr, -dc]))
 
         @pl.when(has[dr, dc])
-        def _(copy=copy):
+        def _():
             copy.start()
+
+        return n
+
+    def arrived(n):
+        copy, _, comes = copies[n]
+
+        @pl.when(comes)
+        def _():
+            copy.wait_recv()
+
+    waits = ([], [])
+    for dc in (-1, 1):
+        waits[0].append(send(0, dc, strips.at[(1 + dc) // 2], sides_in.at[(1 - dc) // 2]))
+    for dr in (-1, 1):
+        for dc in (-1, 1):
+            cells = pl.ds(0, CORNER) if dr < 0 else pl.ds(ROWS * STRIP - CORNER, CORNER)
+            n = send(
+                dr,
+                dc,
+                strips.at[(1 + dc) // 2, cells],
+                corners_in.at[(1 - dr) // 2, (1 - dc) // 2],
+            )
+            waits[1].append(n)
+    for dr in (-1, 1):
+        begin = 0 if dr < 0 else ROWS - HALO
+        n = send(
+            dr,
+            0,
+            features.at[0, pl.ds(begin, HALO)],
+            stage_halo.at[pl.ds(HALO if dr < 0 else 0, HALO), pl.ds(LEFT, COLS)],
+        )
+        waits[1].append(n)
 
     for n in range(4):
         loads[n].wait()
@@ -194,14 +274,6 @@
         @pl.loop(0, 1)
         def _(_, n=n):
             wflat[n] = flipped(wraw[n].reshape(9 * C, C))
-
-    own.wait()
-    for dr, dc in sides:
-        copy = copies[dr, dc]
-
-        @pl.when(has[-dr, -dc])
-        def _(copy=copy):
-            copy.wait_recv()
 
     def silu(dest, values, norm, frame, first):
         for n in range(values.shape[1] // LANES):
@@ -211,25 +283,45 @@
             masked = half * masks[frame, 0:1, place]
             dest[:, place] = (masked * (1.0 + jnp.tanh(half))).astype(BF)
 
-    for first, count in ((HALO, ROWS), (0, HALO), (HALO + ROWS, HALO)):
-        turned = flipped(stage[first : first + count].reshape(count * STAGE, C))
-        for n in range(count):
-            begin = n * STAGE + STRIP - HALO
-            hid_a[:, (first + n) * WIDE : (first + n + 1) * WIDE] = turned[:, begin : begin + WIDE]
-    hid_a[:, TALL * WIDE :] = jnp.zeros((C, hid_a.shape[1] - TALL * WIDE), BF)
-    for n in range(hid_a.shape[1] // TILE):
-        part = slice(n * TILE, (n + 1) * TILE)
-        silu(act_a, hid_a[:, part].astype(F32), 0, 0, n * TILE)
-
-    def conv(layer, source, finish):
-        size = TILES[layer] * TILE
+    def take(part):
+        for n in waits[part]:
+            arrived(n)
+        ref = (stage_own, stage_halo)[part]
+        places = []
+        for first, count, side in PARTS[part]:
+            for n in range(count):
+                at = len(places)
+                for half, place in ((0, LEFT - STRIP), (1, LEFT + COLS)):
+                    if side == 0:
+                        cells = sides_in[half, n * STRIP : (n + 1) * STRIP]
+                    else:
+                        r = n + 1 if side < 0 else n
+                        cells = corners_in[(1 + side) // 2, half, r * STRIP : (r + 1) * STRIP]
+                    ref[at, place : place + STRIP] = cells
+                places.append(first + n)
+        turned = flipped(ref[...].reshape(len(places) * STAGE, C))
+        for at, n in enumerate(places):
+            begin = at * STAGE + LEFT - HALO
+            hid_a[:, n * WIDE : (n + 1) * WIDE] = turned[:, begin : begin + WIDE]
+
+    def first_act(begin, end):
+        silu(act_a, hid_a[:, begin:end].astype(F32), 0, 0, begin)
+
+    def gather(source, begin, end):
         for p in range(3):
             for q in range(3):
                 tap = 3 * p + q
-                patches[tap * C : (tap + 1) * C, 0:size] = source[:, p * WIDE + q : p * WIDE + q + size]
+                shift_by = p * WIDE + q
+                patches[tap * C : (tap + 1) * C, begin:end] = source[:, begin + shift_by : end + shift_by]
+
+    def product(layer, n, finish):
+        part = slice(n * TILE, (n + 1) * TILE)
+        finish(part, jnp.dot(wflat[layer], patches[:, part], preferred_element_type=F32))
+
+    def conv(layer, source, finish):
+        gather(source, 0, TILES[layer] * TILE)
         for n in range(TILES[layer]):
-            part = slice(n * TILE, (n + 1) * TILE)
-            finish(part, jnp.dot(wflat[layer], patches[:, part], preferred_element_type=F32))
+            product(layer, n, finish)
 
     def inner(layer, dest):
         def finish(part, total):
@@ -256,13 +348,28 @@
         size = TILES[layer] * TILE
         dest[:, 0:size] = source[:, 2 * STEP : 2 * STEP + size]
 
+    hid_a[:, TALL * WIDE :] = jnp.zeros((C, hid_a.shape[1] - TALL * WIDE), BF)
+    finish = inner(0, act_b)
+    take(0)
+    first_act(384, 1280)
+    gather(act_a, 512, 1024)
+    product(0, 2, finish)
+    product(0, 3, finish)
+    take(1)
+    first_act(0, 384)
+    first_act(1152, 1792)
+    gather(act_a, 0, 512)
+    gather(act_a, 1024, 1536)
+    for n in (0, 1, 4, 5):
+        product(0, n, finish)
     shifted(hid_s, hid_a, 1)
-    conv(0, act_a, inner(0, act_b))
     conv(1, act_b, outer(1, hid_s, hid_b, act_a))
     conv(2, act_a, inner(2, act_b))
     shifted(hid_s, hid_b, 3)
     conv(3, act_b, outer(3, hid_s, None, act_a))
 
+    for load in small:
+        load.wait()
     size = eps.shape[2]
     taps[...] = jnp.dot(wout[...].astype(BF), act_a[:, 0 : taps.shape[1]], preferred_element_type=F32)
     total = None
@@ -284,10 +391,9 @@
         device_id_type=MESH,
     )
     swap.start()
-    for dr, dc in sides:
-        copy = copies[dr, dc]
-
-        @pl.when(has[dr, dc])
+    for copy, goes, _ in copies:
+
+        @pl.when(goes)
         def _(copy=copy):
             copy.wait_send()
 
@@ -320,7 +426,6 @@
 ):
     hbm = pl.BlockSpec(memory_space=pl.ANY)
     vmem = pl.BlockSpec(memory_space=pltpu.VMEM)
-    smem = pl.BlockSpec(memory_space=pltpu.SMEM)
     dma = pltpu.SemaphoreType.DMA
     lanes = 1792
     def swapped(value):
@@ -328,11 +433,28 @@
 
     result = pl.pallas_call(
         kernel,
-        out_shape=jax.ShapeDtypeStruct((ROWS, 2, COLS), F32),
-        in_specs=[hbm, hbm] + [vmem] * 8 + [smem] * 4,
+        out_shape=pltpu.VMEM((ROWS, 2, COLS), F32),
+        in_specs=[hbm] * 14,
         out_specs=vmem,
         scratch_shapes=[
-            pltpu.VMEM((TALL, STAGE, C), BF),
+            pltpu.VMEM((ROWS, STAGE, C), BF),
+            pltpu.VMEM((2 * HALO, STAGE, C), BF),
+            pltpu.VMEM((2, ROWS * STRIP, C), BF),
+            pltpu.VMEM((2, ROWS * STRIP, C), BF),
+            pltpu.VMEM((2, 2, CORNER, C), BF),
+            pltpu.SMEM((1,), F32),
+            pltpu.SMEM((1,), jnp.int32),
+            pltpu.SMEM((2, 50), F32),
+            pltpu.SMEM((4,), F32),
+            pltpu.VMEM((ROWS, 2, COLS), F32),
+            pltpu.VMEM((2, 2, C), F32),
+            pltpu.VMEM((5, C), F32),
+            pltpu.VMEM((5, C), F32),
+            pltpu.VMEM((1, 2, C), F32),
+            pltpu.VMEM((5, 1, GROUPS), F32),
+            pltpu.VMEM((5, 1, GROUPS), F32),
+            pltpu.VMEM((9, 4, C), BF),
+            dma((12,)),
             pltpu.VMEM((4, 9, C, C), BF),
             pltpu.VMEM((4, C, 9 * C), BF),
             pltpu.VMEM((9 * C, TILES[0] * TILE), BF),
@@ -364,6 +486,10 @@
     )(
         features,
         conv_weight,
+        guidance,
+        timestep,
+        jnp.transpose(coeffs),
+        out_bias,
         swapped(latent),
         conv_bias,
         norm_gain,
@@ -372,10 +498,6 @@
         swapped(stale_mean),
         swapped(stale_var),
         jnp.transpose(out_weight, (0, 2, 1)),
-        out_bias,
-        guidance,
-        timestep,
-        jnp.transpose(coeffs),
     )
     return swapped(result)
 

time: 49.1 us -> 47 us (0.957)
  Pallas kernels: 46 us -> 45 us
  local copies, waits for them, and re-layouts: 1.31 us -> 0.6 us
    pallas_call x1, Pallas kernels: 46 us -> 45 us  [per_device(): pl.pallas_call(kernel, out_shape=pltpu.VMEM((ROWS, 2, COLS), F32), in_spe...]
    unnamed x1, local copies, waits for them, and re-layouts: 1.31 us -> 0.6 us
where the time goes in v3:
time: 47 us; the launch traced here: 46.9 us
  Pallas kernels  45 us (96%)
  between operations  1.31 us (3%)
  local copies, waits for them, and re-layouts  0.6 us (1%)
    pallas_call x1, Pallas kernels, per_device(): pl.pallas_call(kernel, out_shape=pltpu.VMEM((ROWS, 2, COLS), F32), in_spe...  45 us

profile of v3, /device:TPU:6, one launch (start us, length us, event | category | flops | bytes accessed | tf_op | source)
XLA Modules:
  0.0 46.9 jit_solution(16524438895033198518)
XLA Ops:
  1.3 45.0 %shard_map.136 = f32[12,2,64]{2,1,0:T(2,128)S(1)} custom-call(bf16[1,12,64,320]{3,2,1,0:T(8,128)(2,1)} %features.1, bf16[2,2,9,320,320]{4,3,2,1,0:T(8,128)(2,1)} %weight.1, f32[1]{0:T(128)S(6)} %copy.17.guidance_in, s32[1]{0:T(128)S(6)} %copy.18.timestep_in, f32[2,50]{1,0:T(2,128)} %bitcast.11, f32[4]{0:T(128)} %out_bias_in.1, f32[12,2,64]{2,1,0:T(2,128)} %bitcast.8, ...), custom_call_target="tpu_custom_call" | custom-call | flops 12000000000 | bytes 10485760 | tf_op jit(solution)/shard_map/pallas_call | solution.py:434
  46.3 0.6 %copy.16 = f32[2,12,64]{2,0,1:T(2,128)} copy(f32[2,12,64]{2,0,1:T(2,128)S(1)} %bitcast.6) | data formatting | bytes 12288

commit v4 on v3

--- a/solution.py
+++ b/solution.py
@@ -22,9 +22,10 @@
 STEP = WIDE + 1
 TILE = 256
 LANES = 128
-TILES = (6, 6, 5, 5)
+SIZES = (1536, 1408, 1280, 1152)
 GRID_ROWS, GRID_COLS = 16, 16
 NORM_EPS = 1e-05
+MAIN, REST = 256, 64
 
 A_COL, B_COL, BIAS_COL = 0, 5, 10
 
@@ -56,6 +57,8 @@
     strips,
     sides_in,
     corners_in,
+    rest_out,
+    rest_in,
     guidance,
     timestep,
     coeffs,
@@ -107,7 +110,7 @@
 
     @pl.when(edge)
     def _():
-        for ref in (stage_halo, sides_in, corners_in):
+        for ref in (stage_halo, sides_in, corners_in, rest_in):
             ref[...] = jnp.zeros_like(ref)
 
     barrier = pltpu.get_barrier_semaphore()
@@ -152,6 +155,76 @@
         load.start()
         loads.append(load)
 
+    own.wait()
+    for n in range(ROWS):
+        cells = slice(n * STRIP, (n + 1) * STRIP)
+        strips[0, cells] = stage_own[n, LEFT : LEFT + STRIP]
+        strips[1, cells] = stage_own[n, LEFT + COLS - STRIP : LEFT + COLS]
+    for n in range(HALO):
+        for side in range(2):
+            r = n + side * (ROWS - HALO)
+            for half in range(2):
+                begin = LEFT + half * COLS // 2
+                rest_out[side, n, :, half * REST : (half + 1) * REST] = stage_own[
+                    r, begin : begin + COLS // 2, MAIN:C
+                ]
+
+    arrivals = sum(jnp.where(has[s], 1, 0) for s in sides) + 1
+    pl.semaphore_wait(barrier, arrivals)
+
+    copies = []
+
+    def send(dr, dc, source, dest):
+        n = len(copies)
+        copy = pltpu.make_async_remote_copy(
+            src_ref=source,
+            dst_ref=dest,
+            send_sem=send_sem.at[n],
+            recv_sem=recv_sem.at[n],
+            device_id={"row": row + dr, "col": col + dc},
+            device_id_type=MESH,
+        )
+        copies.append((copy, has[dr, dc], has[-dr, -dc]))
+
+        @pl.when(has[dr, dc])
+        def _():
+            copy.start()
+
+        return n
+
+    def arrived(n):
+        copy, _, comes = copies[n]
+
+        @pl.when(comes)
+        def _():
+            copy.wait_recv()
+
+    waits = ([], [])
+    for dc in (-1, 1):
+        waits[0].append(send(0, dc, strips.at[(1 + dc) // 2], sides_in.at[(1 - dc) // 2]))
+    for dr in (-1, 1):
+        for dc in (-1, 1):
+            cells = pl.ds(0, CORNER) if dr < 0 else pl.ds(ROWS * STRIP - CORNER, CORNER)
+            n = send(
+                dr,
+                dc,
+                strips.at[(1 + dc) // 2, cells],
+                corners_in.at[(1 - dr) // 2, (1 - dc) // 2],
+            )
+            waits[1].append(n)
+    for dr in (-1, 1):
+        n = send(dr, 0, rest_out.at[(1 + dr) // 2], rest_in.at[(1 - dr) // 2])
+        waits[1].append(n)
+    for dr in (-1, 1):
+        begin = 0 if dr < 0 else ROWS - HALO
+        n = send(
+            dr,
+            0,
+            features.at[0, pl.ds(begin, HALO), :, pl.ds(0, MAIN)],
+            stage_halo.at[pl.ds(HALO if dr < 0 else 0, HALO), pl.ds(LEFT, COLS), pl.ds(0, MAIN)],
+        )
+        waits[1].append(n)
+
     for load in early:
         load.wait()
     groups = lax.broadcasted_iota(jnp.int32, (GROUPS, C), 0)
@@ -209,65 +282,6 @@
             eye, value, (((1,), (1,)), ((), ())), preferred_element_type=F32
         ).astype(BF)
 
-    own.wait()
-    for n in range(ROWS):
-        cells = slice(n * STRIP, (n + 1) * STRIP)
-        strips[0, cells] = stage_own[n, LEFT : LEFT + STRIP]
-        strips[1, cells] = stage_own[n, LEFT + COLS - STRIP : LEFT + COLS]
-
-    arrivals = sum(jnp.where(has[s], 1, 0) for s in sides) + 1
-    pl.semaphore_wait(barrier, arrivals)
-
-    copies = []
-
-    def send(dr, dc, source, dest):
-        n = len(copies)
-        copy = pltpu.make_async_remote_copy(
-            src_ref=source,
-            dst_ref=dest,
-            send_sem=send_sem.at[n],
-            recv_sem=recv_sem.at[n],
-            device_id={"row": row + dr, "col": col + dc},
-            device_id_type=MESH,
-        )
-        copies.append((copy, has[dr, dc], has[-dr, -dc]))
-
-        @pl.when(has[dr, dc])
-        def _():
-            copy.start()
-
-        return n
-
-    def arrived(n):
-        copy, _, comes = copies[n]
-
-        @pl.when(comes)
-        def _():
-            copy.wait_recv()
-
-    waits = ([], [])
-    for dc in (-1, 1):
-        waits[0].append(send(0, dc, strips.at[(1 + dc) // 2], sides_in.at[(1 - dc) // 2]))
-    for dr in (-1, 1):
-        for dc in (-1, 1):
-            cells = pl.ds(0, CORNER) if dr < 0 else pl.ds(ROWS * STRIP - CORNER, CORNER)
-            n = send(
-                dr,
-                dc,
-                strips.at[(1 + dc) // 2, cells],
-                corners_in.at[(1 - dr) // 2, (1 - dc) // 2],
-            )
-            waits[1].append(n)
-    for dr in (-1, 1):
-        begin = 0 if dr < 0 else ROWS - HALO
-        n = send(
-            dr,
-            0,
-            features.at[0, pl.ds(begin, HALO)],
-            stage_halo.at[pl.ds(HALO if dr < 0 else 0, HALO), pl.ds(LEFT, COLS)],
-        )
-        waits[1].append(n)
-
     for n in range(4):
         loads[n].wait()
 
@@ -298,6 +312,11 @@
                         r = n + 1 if side < 0 else n
                         cells = corners_in[(1 + side) // 2, half, r * STRIP : (r + 1) * STRIP]
                     ref[at, place : place + STRIP] = cells
+                for half in range(2 if side else 0):
+                    begin = LEFT + half * COLS // 2
+                    ref[at, begin : begin + COLS // 2, MAIN:C] = rest_in[
+                        (1 + side) // 2, n, :, half * REST : (half + 1) * REST
+                    ]
                 places.append(first + n)
         turned = flipped(ref[...].reshape(len(places) * STAGE, C))
         for at, n in enumerate(places):
@@ -312,15 +331,19 @@
             for q in range(3):
                 tap = 3 * p + q
                 shift_by = p * WIDE + q
-                patches[tap * C : (tap + 1) * C, begin:end] = source[:, begin + shift_by : end + shift_by]
+                wide = end - begin + -(-shift_by // LANES) * LANES
+                cells = source[:, begin : begin + wide]
+                if shift_by:
+                    cells = pltpu.roll(cells, wide - shift_by, 1)
+                patches[tap * C : (tap + 1) * C, begin:end] = cells[:, 0 : end - begin]
 
     def product(layer, n, finish):
-        part = slice(n * TILE, (n + 1) * TILE)
+        part = slice(n * TILE, min((n + 1) * TILE, SIZES[layer]))
         finish(part, jnp.dot(wflat[layer], patches[:, part], preferred_element_type=F32))
 
     def conv(layer, source, finish):
-        gather(source, 0, TILES[layer] * TILE)
-        for n in range(TILES[layer]):
+        gather(source, 0, SIZES[layer])
+        for n in range(-(-SIZES[layer] // TILE)):
             product(layer, n, finish)
 
     def inner(layer, dest):
@@ -333,7 +356,7 @@
         k = layer // 2
 
         def finish(part, total):
-            for n in range(TILE // LANES):
+            for n in range(total.shape[1] // LANES):
                 place = slice(part.start + n * LANES, part.start + (n + 1) * LANES)
                 skip = before[:, place].astype(F32)
                 inc = total[:, n * LANES : (n + 1) * LANES] + pcols[BIAS_COL + k]
@@ -345,7 +368,7 @@
         return finish
 
     def shifted(dest, source, layer):
-        size = TILES[layer] * TILE
+        size = SIZES[layer]
         dest[:, 0:size] = source[:, 2 * STEP : 2 * STEP + size]
 
     hid_a[:, TALL * WIDE :] = jnp.zeros((C, hid_a.shape[1] - TALL * WIDE), BF)
@@ -442,6 +465,8 @@
             pltpu.VMEM((2, ROWS * STRIP, C), BF),
             pltpu.VMEM((2, ROWS * STRIP, C), BF),
             pltpu.VMEM((2, 2, CORNER, C), BF),
+            pltpu.VMEM((2, HALO, COLS // 2, 2 * REST), BF),
+            pltpu.VMEM((2, HALO, COLS // 2, 2 * REST), BF),
             pltpu.SMEM((1,), F32),
             pltpu.SMEM((1,), jnp.int32),
             pltpu.SMEM((2, 50), F32),
@@ -457,7 +482,7 @@
             dma((12,)),
             pltpu.VMEM((4, 9, C, C), BF),
             pltpu.VMEM((4, C, 9 * C), BF),
-            pltpu.VMEM((9 * C, TILES[0] * TILE), BF),
+            pltpu.VMEM((9 * C, SIZES[0]), BF),
             pltpu.VMEM((C, lanes), BF),
             pltpu.VMEM((C, lanes), BF),
             pltpu.VMEM((C, lanes), BF),
@@ -472,8 +497,8 @@
             pltpu.VMEM((2, 896), F32),
             dma,
             dma((4,)),
-            dma((8,)),
-            dma((8,)),
+            dma((10,)),
+            dma((10,)),
             dma,
             dma,
         ],

time: 47 us -> 44.7 us (0.951)
  Pallas kernels: 45 us -> 42.6 us
    pallas_call x1, Pallas kernels: 45 us -> 42.6 us  [per_device(): pl.pallas_call(kernel, out_shape=pltpu.VMEM((ROWS, 2, COLS), F32), in_spe...]
where the time goes in v4:
time: 44.7 us; the launch traced here: 44.5 us
  Pallas kernels  42.6 us (95%)
  between operations  1.31 us (3%)
  local copies, waits for them, and re-layouts  0.6 us (1%)
    pallas_call x1, Pallas kernels, per_device(): pl.pallas_call(kernel, out_shape=pltpu.VMEM((ROWS, 2, COLS), F32), in_spe...  42.6 us

profile of v4, /device:TPU:6, one launch (start us, length us, event | category | flops | bytes accessed | tf_op | source)
XLA Modules:
  0.0 44.5 jit_solution(1822957174902501870)
XLA Ops:
  1.3 42.6 %shard_map.136 = f32[12,2,64]{2,1,0:T(2,128)S(1)} custom-call(bf16[1,12,64,320]{3,2,1,0:T(8,128)(2,1)} %features.1, bf16[2,2,9,320,320]{4,3,2,1,0:T(8,128)(2,1)} %weight.1, f32[1]{0:T(128)S(6)} %copy.17.guidance_in, s32[1]{0:T(128)S(6)} %copy.18.timestep_in, f32[2,50]{1,0:T(2,128)} %bitcast.11, f32[4]{0:T(128)} %out_bias_in.1, f32[12,2,64]{2,1,0:T(2,128)} %bitcast.8, ...), custom_call_target="tpu_custom_call" | custom-call | flops 12000000000 | bytes 10485760 | tf_op jit(solution)/shard_map/pallas_call | solution.py:457
  43.9 0.6 %copy.16 = f32[2,12,64]{2,0,1:T(2,128)} copy(f32[2,12,64]{2,0,1:T(2,128)S(1)} %bitcast.6) | data formatting | bytes 12288

commit v5 on v4

--- a/solution.py
+++ b/solution.py
@@ -18,7 +18,12 @@
 LEFT = 16
 STAGE = COLS + 2 * LEFT
 CORNER = 6 * STRIP
-PARTS = (((HALO, ROWS, 0),), ((0, HALO, -1), (HALO + ROWS, HALO, 1)))
+NEAR = (2, 3)
+PARTS = (
+    ((HALO, ROWS, 0),),
+    ((HALO - NEAR[0], NEAR[0], -1), (HALO + ROWS, NEAR[1], 1)),
+    ((0, HALO - NEAR[0], -1), (HALO + ROWS + NEAR[1], HALO - NEAR[1], 1)),
+)
 STEP = WIDE + 1
 TILE = 256
 LANES = 128
@@ -53,7 +58,8 @@
     out_weight_in,
     out,
     stage_own,
-    stage_halo,
+    stage_near,
+    stage_far,
     strips,
     sides_in,
     corners_in,
@@ -110,7 +116,7 @@
 
     @pl.when(edge)
     def _():
-        for ref in (stage_halo, sides_in, corners_in, rest_in):
+        for ref in (stage_near, stage_far, sides_in, corners_in, rest_in):
             ref[...] = jnp.zeros_like(ref)
 
     barrier = pltpu.get_barrier_semaphore()
@@ -199,9 +205,25 @@
         def _():
             copy.wait_recv()
 
-    waits = ([], [])
+    waits = ([], [], [])
     for dc in (-1, 1):
         waits[0].append(send(0, dc, strips.at[(1 + dc) // 2], sides_in.at[(1 - dc) // 2]))
+
+    def send_rows(part):
+        place = 0
+        for first, count, side in PARTS[part]:
+            row_out = first + ROWS - HALO if side < 0 else first - ROWS - HALO
+            line = pl.ds(first if side < 0 else first - ROWS - HALO, count)
+            stage = (stage_own, stage_near, stage_far)[part]
+            source = features.at[0, pl.ds(row_out, count), :, pl.ds(0, MAIN)]
+            dest = stage.at[pl.ds(place, count), pl.ds(LEFT, COLS), pl.ds(0, MAIN)]
+            waits[part].append(send(-side, 0, source, dest))
+            place += count
+            source = rest_out.at[(1 - side) // 2, line]
+            dest = rest_in.at[(1 + side) // 2, line]
+            waits[part].append(send(-side, 0, source, dest))
+
+    send_rows(1)
     for dr in (-1, 1):
         for dc in (-1, 1):
             cells = pl.ds(0, CORNER) if dr < 0 else pl.ds(ROWS * STRIP - CORNER, CORNER)
@@ -212,18 +234,7 @@
                 corners_in.at[(1 - dr) // 2, (1 - dc) // 2],
             )
             waits[1].append(n)
-    for dr in (-1, 1):
-        n = send(dr, 0, rest_out.at[(1 + dr) // 2], rest_in.at[(1 - dr) // 2])
-        waits[1].append(n)
-    for dr in (-1, 1):
-        begin = 0 if dr < 0 else ROWS - HALO
-        n = send(
-            dr,
-            0,
-            features.at[0, pl.ds(begin, HALO), :, pl.ds(0, MAIN)],
-            stage_halo.at[pl.ds(HALO if dr < 0 else 0, HALO), pl.ds(LEFT, COLS), pl.ds(0, MAIN)],
-        )
-        waits[1].append(n)
+    send_rows(2)
 
     for load in early:
         load.wait()
@@ -300,7 +311,7 @@
     def take(part):
         for n in waits[part]:
             arrived(n)
-        ref = (stage_own, stage_halo)[part]
+        ref = (stage_own, stage_near, stage_far)[part]
         places = []
         for first, count, side in PARTS[part]:
             for n in range(count):
@@ -309,13 +320,14 @@
                     if side == 0:
                         cells = sides_in[half, n * STRIP : (n + 1) * STRIP]
                     else:
-                        r = n + 1 if side < 0 else n
+                        line = first + n if side < 0 else first + n - HALO - ROWS
+                        r = line + 1 if side < 0 else line
                         cells = corners_in[(1 + side) // 2, half, r * STRIP : (r + 1) * STRIP]
                     ref[at, place : place + STRIP] = cells
                 for half in range(2 if side else 0):
                     begin = LEFT + half * COLS // 2
                     ref[at, begin : begin + COLS // 2, MAIN:C] = rest_in[
-                        (1 + side) // 2, n, :, half * REST : (half + 1) * REST
+                        (1 + side) // 2, line, :, half * REST : (half + 1) * REST
                     ]
                 places.append(first + n)
         turned = flipped(ref[...].reshape(len(places) * STAGE, C))
@@ -379,12 +391,19 @@
     product(0, 2, finish)
     product(0, 3, finish)
     take(1)
-    first_act(0, 384)
-    first_act(1152, 1792)
-    gather(act_a, 0, 512)
-    gather(act_a, 1024, 1536)
-    for n in (0, 1, 4, 5):
-        product(0, n, finish)
+    first_act(256, 384)
+    first_act(1152, 1536)
+    gather(act_a, 256, 512)
+    gather(act_a, 1024, 1280)
+    product(0, 1, finish)
+    product(0, 4, finish)
+    take(2)
+    first_act(0, 256)
+    first_act(1408, 1792)
+    gather(act_a, 0, 256)
+    gather(act_a, 1280, 1536)
+    product(0, 0, finish)
+    product(0, 5, finish)
     shifted(hid_s, hid_a, 1)
     conv(1, act_b, outer(1, hid_s, hid_b, act_a))
     conv(2, act_a, inner(2, act_b))
@@ -461,7 +480,8 @@
         out_specs=vmem,
         scratch_shapes=[
             pltpu.VMEM((ROWS, STAGE, C), BF),
-            pltpu.VMEM((2 * HALO, STAGE, C), BF),
+            pltpu.VMEM((HALO, STAGE, C), BF),
+            pltpu.VMEM((HALO, STAGE, C), BF),
             pltpu.VMEM((2, ROWS * STRIP, C), BF),
             pltpu.VMEM((2, ROWS * STRIP, C), BF),
             pltpu.VMEM((2, 2, CORNER, C), BF),
@@ -497,8 +517,8 @@
             pltpu.VMEM((2, 896), F32),
             dma,
             dma((4,)),
-            dma((10,)),
-            dma((10,)),
+            dma((14,)),
+            dma((14,)),
             dma,
             dma,
         ],

time: 44.7 us -> 44.9 us (level)
  no operation moved by 1% of the time
where the time goes in v5:
time: 44.9 us; the launch traced here: 44.8 us
  Pallas kernels  42.9 us (96%)
  between operations  1.31 us (3%)
  local copies, waits for them, and re-layouts  0.6 us (1%)
    pallas_call x1, Pallas kernels, per_device(): pl.pallas_call(kernel, out_shape=pltpu.VMEM((ROWS, 2, COLS), F32), in_spe...  42.9 us

profile of v5, /device:TPU:6, one launch (start us, length us, event | category | flops | bytes accessed | tf_op | source)
XLA Modules:
  0.0 44.8 jit_solution(7090442248469780537)
XLA Ops:
  1.3 42.9 %shard_map.136 = f32[12,2,64]{2,1,0:T(2,128)S(1)} custom-call(bf16[1,12,64,320]{3,2,1,0:T(8,128)(2,1)} %features.1, bf16[2,2,9,320,320]{4,3,2,1,0:T(8,128)(2,1)} %weight.1, f32[1]{0:T(128)S(6)} %copy.17.guidance_in, s32[1]{0:T(128)S(6)} %copy.18.timestep_in, f32[2,50]{1,0:T(2,128)} %bitcast.11, f32[4]{0:T(128)} %out_bias_in.1, f32[12,2,64]{2,1,0:T(2,128)} %bitcast.8, ...), custom_call_target="tpu_custom_call" | custom-call | flops 12000000000 | bytes 10485760 | tf_op jit(solution)/shard_map/pallas_call | solution.py:476
  44.2 0.6 %copy.16 = f32[2,12,64]{2,0,1:T(2,128)} copy(f32[2,12,64]{2,0,1:T(2,128)S(1)} %bitcast.6) | data formatting | bytes 12288

commit v6 on v4

--- a/solution.py
+++ b/solution.py
@@ -155,6 +155,20 @@
         load.start()
         loads.append(load)
 
+    for n in range(5):
+        cell = lax.broadcasted_iota(jnp.int32, (8, masks.shape[2]), 1) + n * STEP
+        cell_row = lax.shift_right_logical(cell * 28340, 21)
+        cell_col = cell - cell_row * WIDE
+        grid_row = cell_row + (row * ROWS - HALO)
+        grid_col = cell_col + (col * COLS - HALO)
+        inside = (
+            (grid_row >= 0)
+            & (grid_row < GRID_ROWS * ROWS)
+            & (grid_col >= 0)
+            & (grid_col < GRID_COLS * COLS)
+        )
+        masks[n] = jnp.where(inside, 1.0, 0.0).astype(F32)
+
     own.wait()
     for n in range(ROWS):
         cells = slice(n * STRIP, (n + 1) * STRIP)
@@ -168,6 +182,40 @@
                 rest_out[side, n, :, half * REST : (half + 1) * REST] = stage_own[
                     r, begin : begin + COLS // 2, MAIN:C
                 ]
+
+    for load in early:
+        load.wait()
+    groups = lax.broadcasted_iota(jnp.int32, (GROUPS, C), 0)
+    channels = lax.broadcasted_iota(jnp.int32, (GROUPS, C), 1)
+    lowest = groups * (C // GROUPS)
+    spread = jnp.where((channels >= lowest) & (channels < lowest + C // GROUPS), 1.0, 0.0).astype(F32)
+
+    def to_channels(value):
+        total = None
+        for part in exact_parts(value):
+            term = jnp.dot(part, spread, preferred_element_type=F32)
+            total = term if total is None else total + term
+        return total
+
+    scale = to_channels(lax.rsqrt(var[:, 0, :] + NORM_EPS)) * gain[...]
+    offset = shift[...] - to_channels(mean[:, 0, :]) * scale
+    params[...] = jnp.zeros_like(params)
+    for n in range(5):
+        add = offset[n : n + 1]
+        if n in (1, 3):
+            k = n // 2
+            add = add + scale[n : n + 1] * (bias[k, 0:1] + emb[0, k : k + 1])
+        params[A_COL + n : A_COL + n + 1, 0:C] = 0.5 * scale[n : n + 1]
+        params[B_COL + n : B_COL + n + 1, 0:C] = 0.5 * add
+    for k in range(2):
+        params[BIAS_COL + k : BIAS_COL + k + 1, 0:C] = bias[k, 1:2]
+    turned_params = jnp.transpose(params[...])
+    for n in range(12):
+        pcols[n] = jnp.broadcast_to(turned_params[0:C, n : n + 1], (C, LANES))
+
+    wout[...] = jnp.zeros_like(wout)
+    for t in range(9):
+        wout[8 * t : 8 * t + 4, :] = out_weight[t].astype(F32)
 
     arrivals = sum(jnp.where(has[s], 1, 0) for s in sides) + 1
     pl.semaphore_wait(barrier, arrivals)
@@ -225,54 +273,6 @@
         )
         waits[1].append(n)
 
-    for load in early:
-        load.wait()
-    groups = lax.broadcasted_iota(jnp.int32, (GROUPS, C), 0)
-    channels = lax.broadcasted_iota(jnp.int32, (GROUPS, C), 1)
-    lowest = groups * (C // GROUPS)
-    spread = jnp.where((channels >= lowest) & (channels < lowest + C // GROUPS), 1.0, 0.0).astype(F32)
-
-    def to_channels(value):
-        total = None
-        for part in exact_parts(value):
-            term = jnp.dot(part, spread, preferred_element_type=F32)
-            total = term if total is None else total + term
-        return total
-
-    scale = to_channels(lax.rsqrt(var[:, 0, :] + NORM_EPS)) * gain[...]
-    offset = shift[...] - to_channels(mean[:, 0, :]) * scale
-    params[...] = jnp.zeros_like(params)
-    for n in range(5):
-        add = offset[n : n + 1]
-        if n in (1, 3):
-            k = n // 2
-            add = add + scale[n : n + 1] * (bias[k, 0:1] + emb[0, k : k + 1])
-        params[A_COL + n : A_COL + n + 1, 0:C] = 0.5 * scale[n : n + 1]
-        params[B_COL + n : B_COL + n + 1, 0:C] = 0.5 * add
-    for k in range(2):
-        params[BIAS_COL + k : BIAS_COL + k + 1, 0:C] = bias[k, 1:2]
-    turned_params = jnp.transpose(params[...])
-    for n in range(12):
-        pcols[n] = jnp.broadcast_to(turned_params[0:C, n : n + 1], (C, LANES))
-
-    wout[...] = jnp.zeros_like(wout)
-    for t in range(9):
-        wout[8 * t : 8 * t + 4, :] = out_weight[t].astype(F32)
-
-    for n in range(5):
-        cell = lax.broadcasted_iota(jnp.int32, (8, masks.shape[2]), 1) + n * STEP
-        cell_row = lax.shift_right_logical(cell * 28340, 21)
-        cell_col = cell - cell_row * WIDE
-        grid_row = cell_row + (row * ROWS - HALO)
-        grid_col = cell_col + (col * COLS - HALO)
-        inside = (
-            (grid_row >= 0)
-            & (grid_row < GRID_ROWS * ROWS)
-            & (grid_col >= 0)
-            & (grid_col < GRID_COLS * COLS)
-        )
-        masks[n] = jnp.where(inside, 1.0, 0.0).astype(F32)
-
     eye_row = lax.broadcasted_iota(jnp.int32, (C, C), 0)
     eye_col = lax.broadcasted_iota(jnp.int32, (C, C), 1)
     eye = jnp.where(eye_row == eye_col, 1.0, 0.0).astype(BF)
@@ -369,7 +369,9 @@
 
     def shifted(dest, source, layer):
         size = SIZES[layer]
-        dest[:, 0:size] = source[:, 2 * STEP : 2 * STEP + size]
+        wide = size + 2 * LANES
+        cells = pltpu.roll(source[:, 0:wide], wide - 2 * STEP, 1)
+        dest[:, 0:size] = cells[:, 0:size]
 
     hid_a[:, TALL * WIDE :] = jnp.zeros((C, hid_a.shape[1] - TALL * WIDE), BF)
     finish = inner(0, act_b)

time: 44.7 us -> 45 us (level)
  no operation moved by 1% of the time
where the time goes in v6:
time: 45 us; the launch traced here: 44.8 us
  Pallas kernels  42.9 us (95%)
  between operations  1.31 us (3%)
  local copies, waits for them, and re-layouts  0.6 us (1%)
    pallas_call x1, Pallas kernels, per_device(): pl.pallas_call(kernel, out_shape=pltpu.VMEM((ROWS, 2, COLS), F32), in_spe...  42.9 us

profile of v6, /device:TPU:6, one launch (start us, length us, event | category | flops | bytes accessed | tf_op | source)
XLA Modules:
  0.0 44.8 jit_solution(5844737607997911649)
XLA Ops:
  1.3 42.9 %shard_map.136 = f32[12,2,64]{2,1,0:T(2,128)S(1)} custom-call(bf16[1,12,64,320]{3,2,1,0:T(8,128)(2,1)} %features.1, bf16[2,2,9,320,320]{4,3,2,1,0:T(8,128)(2,1)} %weight.1, f32[1]{0:T(128)S(6)} %copy.17.guidance_in, s32[1]{0:T(128)S(6)} %copy.18.timestep_in, f32[2,50]{1,0:T(2,128)} %bitcast.11, f32[4]{0:T(128)} %out_bias_in.1, f32[12,2,64]{2,1,0:T(2,128)} %bitcast.8, ...), custom_call_target="tpu_custom_call" | custom-call | flops 12000000000 | bytes 10485760 | tf_op jit(solution)/shard_map/pallas_call | solution.py:459
  44.2 0.6 %copy.16 = f32[2,12,64]{2,0,1:T(2,128)} copy(f32[2,12,64]{2,0,1:T(2,128)S(1)} %bitcast.6) | data formatting | bytes 12288
